TPU v7x, 128 devices: a whole 4x4x4 slice. The times are simulated.
128 devices in a mesh: reorder: 8 (over z, core), pair: 16 (over y, x).
Axes of the slice: x: 4, y: 4, z: 4, core: 2. Of those that a mesh axis runs over, the one named last changes fastest.
Arguments:
- amps: bfloat16 [16, 16, 16, 4096], P('pair', 'reorder'), may hold values from -3 to 3
- tile_index: int32 [16, 16, 16], replicated, may hold values from 0 to 625, as said below
- ovov: bfloat16 [16, 16, 16, 4096], P('pair', 'reorder'), may hold values from -6 to 6
- cycle_ints: bfloat16 [16, 16, 25, 25, 4096], P('pair', 'reorder'), may hold values from -0.25 to 0.25
- history: bfloat16 [6, 16, 16, 16, 4096], P(None, 'pair', 'reorder'), may hold values from -6 to 6
- slab: int32 [16], replicated, may hold values from 0 to 199, as said below
- eps_occ: float32 [200], replicated, may hold values from -2 to -0.5
- eps_vir: float32 [1600], replicated, may hold values from 0.3 to 4
Outputs:
- new_amps: bfloat16 [16, 16, 16, 4096], P('pair', 'reorder')
- gram_row: float32 [7], replicated
Inputs may be any that keep to these rules, and one draw needn't show every extreme that they name: `tile_index`: entry (i, j, s) is a * 25 + b for the distinct tile (a, b) held in slot s of pair (i, j), or 625 for an empty slot. Live slots come first; each pair has 2 or more. At most 2 live tiles of one pair share a row a, reached. Pairs (i, 2m) and (i, 2m + 1) hold at most 24 live tiles together, reached; some pair holds 16. `slab`: distinct occupied orbitals.
All inputs are finite; a program needn't handle non-finite values.
Results may differ from a plain program's by a relative error of at most 0.008.
Values may be sent and summed in bfloat16 or wider, within the bound.
A program may use at most 128 MiB of HBM per device.

v0:
```python
import jax
import jax.numpy as jnp
from jax import lax
from jax.sharding import PartitionSpec as P

TILE = 64
ROWCAP = 2


def match_lists(out_idx, in_idx, across):
    live_in = in_idx < across * across
    same = ((out_idx // across)[:, None] == (in_idx // across)[None, :]) & live_in[None, :]
    width = in_idx.shape[0]
    ranks = width - jnp.arange(width, dtype=jnp.int32)
    scores = jnp.where(same, ranks[None, :], jnp.zeros_like(ranks)[None, :])
    values, picks = lax.top_k(scores, ROWCAP)
    return (picks, values > 0)


def cycle_block(tiles, in_idx, ints_k, out_idx, out_pair):
    across = ints_k.shape[1]
    slots = out_idx.shape[0]
    picks, present = match_lists(out_idx, in_idx, across)
    cols_in = in_idx % across
    cols_out = out_idx % across
    left = tiles[picks] * present[..., None].astype(tiles.dtype)
    left = (
        left.reshape(slots, ROWCAP, TILE, TILE)
        .transpose(0, 2, 1, 3)
        .reshape(slots, TILE, ROWCAP * TILE)
    )
    right = ints_k[out_pair[:, None], cols_in[picks], cols_out[:, None]]
    right = right.reshape(slots, ROWCAP * TILE, TILE)
    return jnp.einsum("sak,skb->sab", left, right, preferred_element_type=jnp.float32)


def local(amps, tile_index, ovov, cycle_ints, history, slab, eps_occ, eps_vir):
    occ_dev, jdev, capt, tile_area = amps.shape
    ns = tile_index.shape[0]
    across = cycle_ints.shape[2]
    first_here = lax.axis_index("pair") * occ_dev
    second_here = lax.axis_index("reorder") * jdev
    rows_here = lax.all_gather(amps, "reorder", axis=1, tiled=True)
    turned = lax.all_to_all(rows_here, "pair", split_axis=1, concat_axis=0, tiled=True)
    local_idx = lax.dynamic_slice(tile_index, (first_here, second_here, 0), (occ_dev, jdev, capt))
    live = (local_idx < across * across).astype(jnp.float32)

    def cycle_for(first, out_idx, out_pair):
        tiles_i = turned[first]
        in_rows = lax.dynamic_slice_in_dim(tile_index[first], first_here, occ_dev, 0)
        total = cycle_block(tiles_i[0], in_rows[0], cycle_ints[0], out_idx, out_pair)
        return total.reshape(out_idx.shape[0], tile_area)

    def full_row(first):
        out_rows = lax.dynamic_slice_in_dim(tile_index[first], second_here, jdev, 0)
        out_pair = jnp.repeat(jnp.arange(jdev, dtype=jnp.int32), capt)
        return cycle_for(first, out_rows.reshape(-1), out_pair).reshape(jdev, capt, tile_area)

    cycle = lax.psum_scatter(
        jax.vmap(full_row)(jnp.arange(occ_dev * lax.axis_size("pair"), dtype=jnp.int32)).astype(
            jnp.bfloat16
        ),
        "pair",
        scatter_dimension=0,
        tiled=True,
    ).astype(jnp.float32)
    resid = (ovov.astype(jnp.float32) + cycle) * live[..., None]
    occ_pick = (slab[:, None] == jnp.arange(eps_occ.shape[0], dtype=jnp.int32)[None, :]).astype(
        jnp.float32
    )
    occ_energy = jnp.dot(occ_pick, eps_occ, precision=lax.Precision.HIGHEST)
    first_energy = lax.dynamic_slice_in_dim(occ_energy, first_here, occ_dev, 0)
    second_energy = lax.dynamic_slice_in_dim(occ_energy, second_here, jdev, 0)
    vir_tiles = eps_vir.reshape(across, TILE)
    tile_ids = jnp.arange(across, dtype=jnp.int32)
    row_pick = (jnp.minimum(local_idx // across, across - 1)[..., None] == tile_ids).astype(
        jnp.float32
    )
    col_pick = ((local_idx % across)[..., None] == tile_ids).astype(jnp.float32)
    row_energy = jnp.einsum("ijsn,np->ijsp", row_pick, vir_tiles, precision=lax.Precision.HIGHEST)
    col_energy = jnp.einsum("ijsn,np->ijsp", col_pick, vir_tiles, precision=lax.Precision.HIGHEST)
    denom = first_energy[:, None, None, None, None] + second_energy[None, :, None, None, None]
    denom = denom - row_energy[..., :, None] - col_energy[..., None, :]
    denom = denom.reshape(occ_dev, jdev, capt, tile_area)
    new_amps = ((amps.astype(jnp.float32) + resid / denom) * live[..., None]).astype(jnp.bfloat16)
    cross = jnp.einsum(
        "hijsx,ijsx->h",
        history,
        resid,
        precision=lax.Precision.HIGHEST,
        preferred_element_type=jnp.float32,
    )
    square = jnp.sum(resid * resid)
    cross, square = lax.psum((cross, square), ("reorder", "pair"))
    gram_row = jnp.concatenate([cross, jnp.sqrt(square)[None]]) / (TILE * ns)
    return (new_amps, gram_row)


def solution(mesh):
    in_specs = (
        P("pair", "reorder", None, None),
        P(),
        P("pair", "reorder", None, None),
        P("pair", "reorder", None, None, None),
        P(None, "pair", "reorder", None, None),
        P(),
        P(),
        P(),
    )
    out_specs = (P("pair", "reorder", None, None), P())
    return jax.shard_map(local, mesh=mesh, in_specs=in_specs, out_specs=out_specs, check_vma=False)
```

profile of v0, /device:TPU:1, one launch (start us, length us, event | category | flops | bytes accessed | tf_op | source)
XLA Modules:
  0.0 457.6 jit_solution(4550711208892669804)
XLA Ops:
  7.2 0.0 copy-start
  7.2 0.0 all-gather.2.cloned.1.call-start
  7.2 0.7 all-gather.2.cloned.1.call-update
  7.9 1.5 gather_fusion.1
  9.4 0.1 fusion.27
  9.5 0.1 constant_dynamic-slice_fusion.2
  9.6 29.2 %all-gather.2.cloned.1.call-done = bf16[1,16,16,4096]{3,2,0,1:T(8,128)(2,1)} async-done(((bf16[1,2,16,4096]{3,2,0,1:T(8,128)(2,1)}), bf16[1,16,16,4096]{3,2,0,1:T(8,128)(2,1)}) %all-gather.2.cloned.1.call-update) | async-done | bytes 2097168 | tf_op jit(solution)/shard_map/all_gather | solution.py:43
  38.8 6.6 %all-to-all-start = ((bf16[1,16,16,4096]{3,2,0,1:T(8,128)(2,1)}), bf16[1,16,16,4096]{3,2,0,1:T(8,128)(2,1)}, u32[]{:S(2)}, u32[]{:S(2)}) async-start(bf16[1,16,16,4096]{3,2,0,1:T(8,128)(2,1)} %all-gather.2.cloned.1.call-done), calls=%async_computation | async-start | bytes 4194304 | tf_op jit(solution)/shard_map/all_to_all | solution.py:44
  45.4 0.0 reduce-scatter.4.cloned.1.call-start
  45.4 0.1 copy.100
  45.5 0.1 copy.101
  45.6 0.1 copy.74
  45.7 0.1 copy.80
  45.7 0.1 broadcast_compare_fusion
  45.8 0.7 div.50
  46.5 0.1 and_select_fusion
  46.7 1.7 top_k.12
  48.5 0.2 copy.84
  48.6 0.2 reshape.305
  48.8 0.2 copy.85
  49.0 7.1 %gather_fusion.4 = s32[1024]{0:T(1024)S(1)} fusion(s32[16,16]{1,0:T(8,128)S(1)} %get-tuple-element.43, s32[1024]{0:T(1024)S(1)} %reshape.305), kind=kCustom, calls=%fused_computation.4 | custom fusion | bytes 16384 | tf_op jit(solution)/shard_map/vmap()/gather | solution.py:32
  56.1 0.2 gather.33
  56.3 0.2 copy.87
  56.5 0.1 copy.93
  56.5 0.1 reshape.183
  56.7 0.2 copy.94
  56.9 0.2 reshape.299
  57.0 41.9 %gather_fusion.2 = bf16[1024,4096]{1,0:T(8,128)(2,1)} fusion(bf16[2,25,25,4096]{3,0,2,1:T(2,128)(2,1)} %bitcast.102, s32[1024]{0:T(1024)S(1)} %reshape.299), kind=kCustom, calls=%fused_computation.2 | custom fusion | bytes 16789504 | tf_op jit(solution)/shard_map/vmap()/gather | solution.py:32
  98.9 23.6 %reshape.184 = bf16[16,32,128,64]{3,2,1,0:T(8,128)(2,1)} reshape(bf16[1024,4096]{1,0:T(8,128)(2,1)} %gather_fusion.2) | data formatting | bytes 16777216 | tf_op jit(solution)/shard_map/vmap()/reshape | solution.py:33
  122.5 0.0 all-to-all-done
  122.5 3.6 gather_fusion
  126.1 68.5 %gather_fusion.3 = bf16[1024,4096]{1,0:T(8,128)(2,1)} fusion(bf16[16,16,4096]{2,1,0:T(8,128)(2,1)} %gather_fusion, s32[1024]{0:T(1024)S(1)} %reshape.305), kind=kCustom, calls=%fused_computation.3 | custom fusion | bytes 16785408 | tf_op jit(solution)/shard_map/vmap()/gather | solution.py:26
  194.6 23.6 %gather.31 = bf16[16,32,2,64,64]{4,3,2,1,0:T(8,128)(2,1)} reshape(bf16[1024,4096]{1,0:T(8,128)(2,1)} %gather_fusion.3) | data formatting | bytes 16777216 | tf_op jit(solution)/shard_map/vmap()/gather | solution.py:26
  218.2 8.3 %multiply_bitcast_fusion = bf16[16,32,64,2,64]{4,2,3,1,0:T(8,128)(2,1)S(1)} fusion(bf16[16,32,2,64,64]{4,3,2,1,0:T(8,128)(2,1)} %gather.31, bf16[16,32,2]{2,1,0:T(8,128)(2,1)S(1)} %copy.85), kind=kLoop, calls=%fused_computation.5 | loop fusion | flops 4194304 | bytes 16779264 | tf_op jit(solution)/shard_map/vmap()/transpose | solution.py:29
  226.4 16.0 %copy.86 = bf16[16,32,64,2,64]{4,3,2,1,0:T(2,128)(2,1)} copy(bf16[16,32,64,2,64]{4,2,3,1,0:T(8,128)(2,1)S(1)} %multiply_bitcast_fusion) | data formatting | bytes 16777216 | tf_op jit(solution)/shard_map/vmap()/transpose | solution.py:29
  242.4 26.9 %reshape.182 = bf16[16,32,64,128]{3,2,1,0:T(8,128)(2,1)} reshape(bf16[16,32,64,2,64]{4,3,2,1,0:T(2,128)(2,1)} %copy.86) | data formatting | bytes 16777216 | tf_op jit(solution)/shard_map/vmap()/reshape | solution.py:30
  269.3 13.1 %convolution_convert_fusion = bf16[16,32,64,64]{3,2,1,0:T(8,128)(2,1)} fusion(bf16[16,32,64,128]{3,2,1,0:T(8,128)(2,1)} %reshape.182, bf16[16,32,128,64]{3,2,1,0:T(8,128)(2,1)} %reshape.184), kind=kOutput, calls=%fused_computation.6 | convolution fusion | flops 538968064 | bytes 20971520 | tf_op jit(solution)/shard_map/vmap(sak,skb->sab)/dot_general | solution.py:34
  282.4 0.0 copy-start.3
  282.4 0.0 copy-start.4
  282.4 0.0 copy-start.2
  282.4 0.0 copy-start.1
  282.4 12.1 %convert_element_type.30 = bf16[16,2,16,4096]{3,2,1,0:T(8,128)(2,1)} reshape(bf16[16,32,64,64]{3,2,1,0:T(8,128)(2,1)} %convolution_convert_fusion) | data formatting | bytes 8388608 | tf_op jit(solution)/shard_map/convert_element_type | solution.py:60
  294.6 0.0 reduce-scatter.4.cloned.1.call-update
  294.6 0.0 copy-done.3
  294.6 0.0 copy-done.4
  294.6 0.2 convolution_bitcast_fusion
  294.8 0.7 dynamic_slice.10
  295.5 0.0 copy-done.2
  295.5 0.1 reshape.353
  295.5 0.7 dynamic-slice_add_fusion
  296.3 0.7 minimum_bitcast_fusion
  297.0 0.2 fusion.17
  297.1 0.2 convolution_subtract_fusion
  297.3 0.4 broadcast_subtract_fusion
  297.7 0.4 sub.64
  298.1 0.7 fusion.25
  298.8 75.8 %reduce-scatter.4.cloned.1.call-done = bf16[1,2,16,4096]{3,2,1,0:T(8,128)(2,1)} async-done(((bf16[16,2,16,4096]{3,2,1,0:T(8,128)(2,1)}), bf16[1,2,16,4096]{3,2,1,0:T(8,128)(2,1)}) %reduce-scatter.4.cloned.1.call-update) | async-done | bytes 262160
  374.6 0.0 copy-done.1
  374.6 2.6 fusion.6
  377.1 0.0 copy-done
  377.1 6.2 %fusion.2 = f32[6]{0:T(128)S(1)} fusion(bf16[6,2,16,4096]{3,2,1,0:T(8,128)(2,1)S(1)} %bitcast.101, f32[2,16,4096,1]{2,1,0,3:T(8,128)S(1)} %get-tuple-element.34), kind=kOutput, calls=%fused_computation.11 | convolution fusion | flops 9437184 | bytes 2097176 | tf_op jit(solution)/shard_map/hijsx,ijsx->h/dot_general | solution.py:86
  383.3 66.2 %all-reduce.1 = (f32[]{:T(128)}, f32[6]{0:T(128)S(1)}) all-reduce(f32[]{:T(128)} %get-tuple-element.35, f32[6]{0:T(128)S(1)} %fusion.2), channel_id=1, replica_groups=mesh['reorder'=8,'pair'=16] {'reorder','pair'}, use_global_device_ids=true, to_apply=%region_4.5 | all-reduce | flops 7 | bytes 56 | tf_op jit(solution)/shard_map/psum | solution.py:94
  450.2 0.6 maximum_multiply_fusion
  (15 shorter events, 0.2 us)
Async XLA Ops:
  7.2 370.0 %copy-start = (bf16[6,1,2,16,4096]{4,3,2,1,0:T(8,128)(2,1)S(1)}, bf16[6,1,2,16,4096]{4,3,2,1,0:T(8,128)(2,1)}, u32[]{:S(2)}) copy-start(bf16[6,1,2,16,4096]{4,3,2,1,0:T(8,128)(2,1)} %param.12) | copy-start | bytes 4718596
  7.2 31.6 %all-gather.2.cloned.1.call-start = ((), (), s32[]{:S(2)}) async-start(), calls=%async_computation.2 | async-start | bytes 2359296 | tf_op jit(solution)/shard_map/all_gather | solution.py:43
  38.8 83.8 %all-to-all-start = ((bf16[1,16,16,4096]{3,2,0,1:T(8,128)(2,1)}), bf16[1,16,16,4096]{3,2,0,1:T(8,128)(2,1)}, u32[]{:S(2)}, u32[]{:S(2)}) async-start(bf16[1,16,16,4096]{3,2,0,1:T(8,128)(2,1)} %all-gather.2.cloned.1.call-done), calls=%async_computation | async-start | bytes 4194304 | tf_op jit(solution)/shard_map/all_to_all | solution.py:44
  45.4 329.2 %reduce-scatter.4.cloned.1.call-start = ((), (), s32[]{:S(2)}) async-start(), calls=%async_computation.3 | async-start | bytes 4456448
  282.4 12.2 %copy-start.3 = (f32[200]{0:T(256)S(1)}, f32[200]{0:T(256)}, u32[]{:S(2)}) copy-start(f32[200]{0:T(256)} %param.14) | copy-start | bytes 2404
  282.4 12.2 %copy-start.4 = (s32[16]{0:T(128)S(1)}, s32[16]{0:T(128)}, u32[]{:S(2)}) copy-start(s32[16]{0:T(128)} %param.13) | copy-start | bytes 196
  282.4 13.1 %copy-start.2 = (f32[1600]{0:T(1024)S(1)}, f32[1600]{0:T(1024)}, u32[]{:S(2)}) copy-start(f32[1600]{0:T(1024)} %param.15) | copy-start | bytes 19204
  282.4 92.1 %copy-start.1 = (bf16[1,2,16,4096]{3,2,1,0:T(8,128)(2,1)S(1)}, bf16[1,2,16,4096]{3,2,1,0:T(8,128)(2,1)}, u32[]{:S(2)}) copy-start(bf16[1,2,16,4096]{3,2,1,0:T(8,128)(2,1)} %param.8) | copy-start | bytes 786436
Sparse Core Ops, SparseCore 0:
  9.7 28.9 all-gather.1
  294.7 79.7 reduce-scatter.3
where the time goes:
time: 463 us; the launch traced here: 458 us
  local copies, waits for them, and re-layouts  228 us (49%)
  waiting for transfers between devices  106 us (23%)
  blocking collectives  66.2 us (14%)
  matrix products  19.9 us (4%)
  other arithmetic  16.7 us (4%)
  between operations  15 us (3%)
  starting transfers between devices  6.66 us (1%)
    gather x4, local copies, waits for them, and re-layouts, cycle_block(): left = tiles[picks] * present[..., None].astype(tiles.dtype)  92.4 us
    unnamed x3, waiting for transfers between devices  76.5 us
    psum x1, blocking collectives, local(): cross, square = lax.psum((cross, square), ('reorder', 'pair'))  66.2 us
    gather x4, local copies, waits for them, and re-layouts, cycle_block(): right = ints_k[out_pair[:, None], cols_in[picks], cols_out[:, None]]  49.3 us
    all_gather x1, waiting for transfers between devices, local(): rows_here = lax.all_gather(amps, 'reorder', axis=1, tiled=True)  29.2 us
    reshape x1, local copies, waits for them, and re-layouts, cycle_block(): left = left.reshape(slots, ROWCAP, TILE, TILE).transpose(0, 2, 1, 3).resh...  26.9 us
    reshape x1, local copies, waits for them, and re-layouts, cycle_block(): right = right.reshape(slots, ROWCAP * TILE, TILE)  23.6 us
    transpose x1, local copies, waits for them, and re-layouts, cycle_block(): left = left.reshape(slots, ROWCAP, TILE, TILE).transpose(0, 2, 1, 3).resh...  16 us
  transfers between devices with their start and end apart: 3, of which 2 were waited for; matrix products, arithmetic and copies ran while one was open for 18% of the time, Pallas kernels for 0%

commit v1 on v0

v1 whole, which is shorter than its diff:
```python
import jax
import jax.numpy as jnp
from jax import lax
from jax.experimental import pallas as pl
from jax.experimental.pallas import tpu as pltpu
from jax.sharding import PartitionSpec as P

MESH = pl.DeviceIdType.MESH
TILE = 64
HALF = 32
AREA = TILE * TILE
LIVE2 = 24
NP = 16
NR = 8
CAPT = 16
NH = 6
F32, BF16 = jnp.float32, jnp.bfloat16


def iota(shape, dim):
    return lax.broadcasted_iota(jnp.int32, shape, dim)


def kernel(
    jobs, slot_of, amps, live, pair_e, row_e, col_e, ovov_hbm, ints_hbm, hist_hbm,
    new_amps, gram,
    ints, ovov, hist, stage, a_out, a_land, a_exp, mask, parts, c_land, total, cyc, g_one, g_two,
    w_sem, in_sem, a_send, a_recv, c_send, c_recv, g_send, g_recv,
):
    r = lax.axis_index("reorder")
    p = lax.axis_index("pair")
    barrier = pltpu.get_barrier_semaphore()

    def signal(device):
        pl.semaphore_signal(barrier, inc=1, device_id=device, device_id_type=MESH)

    w_copy = pltpu.make_async_copy(ints_hbm, ints, w_sem.at[0])
    w_copy.start()
    ovov_copy = pltpu.make_async_copy(ovov_hbm, ovov, in_sem.at[0])
    ovov_copy.start()
    hist_copy = pltpu.make_async_copy(hist_hbm, hist, in_sem.at[1])
    hist_copy.start()

    def greet_row(d, c):
        signal(((r + d) % NR, p))
        return c

    def greet_pair(d, c):
        signal((r, (p + d) % NP))
        return c

    own = p // 2 == r

    def greet_amps(i, c):
        @pl.when(jnp.logical_not(jnp.logical_and(own, i == p)))
        def _():
            signal((p // 2, i))

        return c

    lax.fori_loop(1, NR, greet_row, 0)
    lax.fori_loop(1, NP, greet_pair, 0)
    lax.fori_loop(0, NP, greet_amps, 0)

    lane_in, lane_out = iota((128, 128), 0), iota((128, 128), 1)
    half, q = lane_in // TILE, lane_in % TILE
    order = (lane_out == half * TILE + (q % 2) * HALF + q // 2).astype(BF16)

    def turn(m, c):
        x = amps[:, :, pl.ds(pl.multiple_of(m * 128, 128), 128)].reshape(2 * CAPT, 128)
        y = jnp.dot(x, order, preferred_element_type=F32)
        stage[pl.ds(m, 2 * CAPT, stride=HALF), :] = y
        return c

    lax.fori_loop(0, HALF, turn, 0)
    a_out[...] = stage[...].astype(BF16).reshape(2, CAPT * HALF, 128)

    pl.semaphore_wait(barrier, NR - 1 + NP - 1 + 2 * NR - own.astype(jnp.int32))

    def amps_copy(kk, d):
        return pltpu.make_async_remote_copy(
            src_ref=a_out.at[kk],
            dst_ref=a_land.at[p],
            send_sem=a_send.at[kk * NR + d],
            recv_sem=a_recv.at[p],
            device_id=((r + d) % NR, 2 * r + kk),
            device_id_type=MESH,
        )

    def to_other(kk, d):
        return jnp.logical_not(jnp.logical_and(d == 0, 2 * r + kk == p))

    def send_amps(n, c):
        @pl.when(to_other(n % 2, n // 2))
        def _():
            amps_copy(n % 2, n // 2).start()

        return c

    lax.fori_loop(0, 2 * NR, send_amps, 0)

    @pl.when(own)
    def _():
        a_land[p] = a_out[p % 2]

    lane_in, lane_out = iota((128, 256), 0), iota((128, 256), 1)
    spread = (lane_in == lane_out // 2).astype(BF16)
    lane = iota((CAPT, 128), 1)
    mask[0] = (lane % 2 == 0).astype(BF16)
    mask[1] = (lane % 2 == 1).astype(BF16)
    mask[2] = jnp.zeros((CAPT, 128), BF16)
    low = iota((1, 128), 1) < TILE
    low_f = (iota((TILE, 128), 1) < TILE).astype(F32)
    keep = (low_f.astype(BF16), (1.0 - low_f).astype(BF16))
    low = iota((HALF, 128), 1) < TILE

    w_copy.wait()

    def parts_copy(i):
        return pltpu.make_async_remote_copy(
            src_ref=parts.at[i],
            dst_ref=c_land.at[p],
            send_sem=c_send.at[i],
            recv_sem=c_recv.at[p],
            device_id=(r, i),
            device_id_type=MESH,
        )

    def one_first(n, c):
        i = (p + 1 + n) % NP

        @pl.when(jnp.logical_not(jnp.logical_and(own, i == p)))
        def _():
            pltpu.make_async_copy(a_land.at[i], a_land.at[i], a_recv.at[i]).wait()

        wide = jnp.dot(a_land[i], spread, preferred_element_type=F32).astype(BF16)
        a_exp[:, :HALF, :] = wide[:, :128].reshape(CAPT, HALF, 128)
        a_exp[:, HALF:, :] = wide[:, 128:].reshape(CAPT, HALF, 128)

        def job(u, c):
            rows, cols = [], []
            for side in range(2):
                code = jobs[side, i, u]
                tile, sel, at = code // 4 % CAPT, code % 4, code // (4 * CAPT)
                x = a_exp[tile].reshape(4, CAPT, 128) * mask[sel][None]
                rows.append(x.reshape(TILE, 128))
                w = ints[at]
                cols += [w * keep[0], w * keep[1]]
            out = jnp.dot(
                jnp.concatenate(rows, axis=1),
                jnp.concatenate(cols, axis=0),
                preferred_element_type=F32,
            )
            top, bottom = out[:HALF], out[HALF:]
            both = jnp.where(
                low, top + pltpu.roll(top, TILE, 1), bottom + pltpu.roll(bottom, TILE, 1)
            )
            parts[i, pl.ds(pl.multiple_of(u * HALF, HALF), HALF), :] = both.astype(BF16)
            return c

        lax.fori_loop(0, LIVE2, job, 0, unroll=4)

        @pl.when(i != p)
        def _():
            parts_copy(i).start()

        return c

    lax.fori_loop(0, NP, one_first, 0)

    total[...] = parts[p].astype(F32).reshape(LIVE2, HALF, 128)

    def add(d, c):
        k = (p + NP - d) % NP
        pltpu.make_async_copy(c_land.at[k], c_land.at[k], c_recv.at[k]).wait()
        total[...] += c_land[k].astype(F32).reshape(LIVE2, HALF, 128)
        return c

    lax.fori_loop(1, NP, add, 0)

    def place(s, c):
        cyc[pl.ds(pl.multiple_of(s * HALF, HALF), HALF), :] = total[slot_of[s]]
        return c

    lax.fori_loop(0, 2 * CAPT, place, 0)
    ovov_copy.wait()
    hist_copy.wait()

    alive = jnp.broadcast_to(live[...], (2 * CAPT, 128))
    col = jnp.concatenate([col_e[...], col_e[...]], axis=1)
    base = pair_e[...] - col
    rows = row_e[...]
    pick_q, pick_lane = iota((TILE, 128), 0), iota((TILE, 128), 1) // TILE

    def finish(m, sums):
        at = pl.ds(pl.multiple_of(m * 128, 128), 128)
        cycle = cyc[pl.ds(m, 2 * CAPT, stride=HALF), :]
        ov = ovov[:, :, at].reshape(2 * CAPT, 128).astype(F32)
        resid = (ov + cycle) * alive
        pick = (pick_q == 2 * m + pick_lane).astype(F32)
        row = jnp.dot(rows, pick, precision=lax.Precision.HIGHEST, preferred_element_type=F32)
        old = amps[:, :, at].reshape(2 * CAPT, 128).astype(F32)
        new = (old + resid / (base - row)) * alive
        new_amps[:, :, at] = new.astype(BF16).reshape(2, CAPT, 128)
        terms = [hist[h, :, :, at].reshape(2 * CAPT, 128).astype(F32) for h in range(NH)]
        terms.append(resid)
        return tuple(
            s + (t * resid).reshape(4, 8, 128).sum(axis=0) for s, t in zip(sums, terms)
        )

    zero = jnp.zeros((8, 128), F32)
    sums = lax.fori_loop(0, HALF, finish, (zero,) * (NH + 1))
    at_row = iota((8, 128), 0)
    mine = zero
    for h, s in enumerate(sums):
        mine = jnp.where(at_row == h, jnp.sum(s, axis=0, keepdims=True), mine)

    def row_copy(d):
        return pltpu.make_async_remote_copy(
            src_ref=g_one.at[r], dst_ref=g_one.at[r], send_sem=g_send.at[d],
            recv_sem=g_recv.at[r], device_id=((r + d) % NR, p), device_id_type=MESH,
        )

    def pair_copy(d):
        return pltpu.make_async_remote_copy(
            src_ref=g_two.at[p], dst_ref=g_two.at[p], send_sem=g_send.at[NR + d],
            recv_sem=g_recv.at[NR + p], device_id=(r, (p + d) % NP), device_id_type=MESH,
        )

    def start_all(copy):
        def step(d, c):
            copy(d).start()
            return c

        return step

    def sent_all(copy):
        def step(d, c):
            copy(d).wait_send()
            return c

        return step

    g_one[r] = mine
    lax.fori_loop(1, NR, start_all(row_copy), 0)

    def got_row(d, c):
        k = (r + NR - d) % NR
        pltpu.make_async_copy(g_one.at[k], g_one.at[k], g_recv.at[k]).wait()
        return c

    lax.fori_loop(1, NR, got_row, 0)
    g_two[p] = jnp.sum(g_one[...], axis=0)
    lax.fori_loop(1, NP, start_all(pair_copy), 0)

    def got_pair(d, c):
        k = (p + NP - d) % NP
        pltpu.make_async_copy(g_two.at[k], g_two.at[k], g_recv.at[NR + k]).wait()
        return c

    lax.fori_loop(1, NP, got_pair, 0)
    everyone = jnp.sum(jnp.sum(g_two[...], axis=0), axis=1, keepdims=True)
    everyone = jnp.broadcast_to(everyone, (8, 128))
    gram[...] = jnp.where(at_row == NH, jnp.sqrt(everyone), everyone) / (TILE * NP)

    lax.fori_loop(1, NR, sent_all(row_copy), 0)
    lax.fori_loop(1, NP, sent_all(pair_copy), 0)

    def sent_parts(d, c):
        parts_copy((p + d) % NP).wait_send()
        return c

    lax.fori_loop(1, NP, sent_parts, 0)

    def sent_amps(n, c):
        @pl.when(to_other(n % 2, n // 2))
        def _():
            amps_copy(n % 2, n // 2).wait_send()

        return c

    lax.fori_loop(0, 2 * NR, sent_amps, 0)


def tables(tile_index, first, second, across):
    dead = across * across
    ns, _, capt = tile_index.shape
    t = jnp.arange(capt, dtype=jnp.int32)
    inner = lax.dynamic_slice(tile_index, (0, first, 0), (ns, 1, capt))
    outer = lax.dynamic_slice(tile_index, (0, second, 0), (ns, 2, capt))
    count = jnp.sum((outer[:, :1] < dead).astype(jnp.int32), axis=2, keepdims=True)
    shift = jnp.concatenate([jnp.zeros_like(count), count], axis=1)
    place = jnp.where(outer < dead, t + shift, -1).reshape(ns, 1, 2 * capt)
    u = jnp.arange(LIVE2, dtype=jnp.int32)[None, :, None]
    packed = jnp.sum(
        jnp.where(place == u, outer.reshape(ns, 1, 2 * capt) - dead, 0), axis=2, keepdims=True
    ) + dead
    which = (u >= count).astype(jnp.int32)
    same = (packed // across == inner // across) & (inner < dead)
    none = dead * capt
    code = (inner % across) * across * capt + t
    lowest = jnp.min(jnp.where(same, t, capt), axis=2, keepdims=True)
    highest = jnp.max(jnp.where(same, t, -1), axis=2, keepdims=True)

    def entry(pick, present):
        found = jnp.sum(jnp.where(t == pick, code, 0), axis=2, keepdims=True)
        found = found + (packed % across) * capt
        return jnp.where(present, found * 4 + which, 2)[..., 0]

    jobs = jnp.stack([entry(lowest, lowest < capt), entry(highest, highest > lowest)])
    return jobs


def local(amps, tile_index, ovov, cycle_ints, history, slab, eps_occ, eps_vir):
    _, jdev, capt, area = amps.shape
    across = cycle_ints.shape[2]
    dead = across * across
    p = lax.axis_index("pair")
    r = lax.axis_index("reorder")
    jobs = tables(tile_index, p, r * jdev, across)
    local_idx = lax.dynamic_slice(tile_index, (p, r * jdev, 0), (1, jdev, capt))[0]
    slots = jnp.arange(capt, dtype=jnp.int32)
    count = jnp.sum((local_idx[0] < dead).astype(jnp.int32))
    slot_of = jnp.concatenate([slots, jnp.minimum(slots + count, LIVE2 - 1)])
    flat = local_idx.reshape(-1)
    live = (flat < dead).astype(F32)[:, None]
    occ = eps_occ[slab]
    pair_e = lax.dynamic_slice(occ, (p,), (1,)) + jnp.repeat(
        lax.dynamic_slice(occ, (r * jdev,), (jdev,)), capt
    )
    vir = eps_vir.reshape(across, TILE)
    row_e = vir[jnp.minimum(flat // across, across - 1)]
    col_e = vir[flat % across]
    ints = cycle_ints[0].transpose(1, 2, 0, 3).reshape(dead, 2, HALF, 128)
    ints = ints.transpose(0, 2, 1, 3).reshape(dead, TILE, 128)

    vmem = pl.BlockSpec(memory_space=pltpu.VMEM)
    smem = pl.BlockSpec(memory_space=pltpu.SMEM)
    hbm = pl.BlockSpec(memory_space=pl.ANY)
    dma = pltpu.SemaphoreType.DMA
    new_amps, gram = pl.pallas_call(
        kernel,
        out_shape=(
            jax.ShapeDtypeStruct((jdev, capt, area), BF16),
            jax.ShapeDtypeStruct((8, 128), F32),
        ),
        in_specs=[smem, smem, vmem, vmem, vmem, vmem, vmem, hbm, hbm, hbm],
        out_specs=(vmem, vmem),
        scratch_shapes=[
            pltpu.VMEM((dead, TILE, 128), BF16),
            pltpu.VMEM((jdev, capt, area), BF16),
            pltpu.VMEM((NH, jdev, capt, area), BF16),
            pltpu.VMEM((2 * capt * HALF, 128), F32),
            pltpu.VMEM((2, capt * HALF, 128), BF16),
            pltpu.VMEM((NP, capt * HALF, 128), BF16),
            pltpu.VMEM((capt, TILE, 128), BF16),
            pltpu.VMEM((3, capt, 128), BF16),
            pltpu.VMEM((NP, LIVE2 * HALF, 128), BF16),
            pltpu.VMEM((NP, LIVE2 * HALF, 128), BF16),
            pltpu.VMEM((LIVE2, HALF, 128), F32),
            pltpu.VMEM((2 * capt * HALF, 128), F32),
            pltpu.VMEM((NR, 8, 128), F32),
            pltpu.VMEM((NP, 8, 128), F32),
            dma((1,)),
            dma((2,)),
            dma((2 * NR,)),
            dma((NP,)),
            dma((NP,)),
            dma((NP,)),
            dma((NR + NP,)),
            dma((NR + NP,)),
        ],
        compiler_params=pltpu.CompilerParams(
            collective_id=0, has_side_effects=True, vmem_limit_bytes=48 << 20
        ),
    )(jobs, slot_of, amps[0], live, pair_e[:, None], row_e, col_e, ovov[0], ints, history[:, 0])
    return new_amps[None], gram[: NH + 1, 0]


def solution(mesh):
    in_specs = (
        P("pair", "reorder", None, None),
        P(),
        P("pair", "reorder", None, None),
        P("pair", "reorder", None, None, None),
        P(None, "pair", "reorder", None, None),
        P(),
        P(),
        P(),
    )
    out_specs = (P("pair", "reorder", None, None), P())
    return jax.shard_map(local, mesh=mesh, in_specs=in_specs, out_specs=out_specs, check_vma=False)
```

time: 463 us -> 199 us (0.43); the launches traced: 458 us -> 199 us
  local copies, waits for them, and re-layouts: 228 us -> 10.2 us
  Pallas kernels: 0 us -> 184 us
  waiting for transfers between devices: 106 us -> 0 us
  blocking collectives: 66.2 us -> 0 us
  matrix products: 19.9 us -> 0 us
  between operations: 15 us -> 0.75 us
  other arithmetic: 16.7 us -> 4.45 us
  starting transfers between devices: 6.66 us -> 0 us
    pallas_call x0 -> x1, Pallas kernels: none -> 184 us  [local(): pl.pallas_call(kernel, out_shape=(jax.ShapeDtypeStruct((jdev, capt, area)...]
    gather x10 -> x3, local copies, waits for them, and re-layouts: 147 us -> 1.81 us  [the longest x1 0.66 us: local(): occ = eps_occ[slab]]
    unnamed x3 -> x0, waiting for transfers between devices: 76.5 us -> none
    psum x1 -> x0, blocking collectives: 66.2 us -> none  [local(): cross, square = lax.psum((cross, square), ('reorder', 'pair'))]
    reshape x4 -> x1, local copies, waits for them, and re-layouts: 50.7 us -> 0.77 us  [local(): vir = eps_vir.reshape(across, TILE)]
    all_gather x1 -> x0, waiting for transfers between devices: 29.2 us -> none  [local(): rows_here = lax.all_gather(amps, 'reorder', axis=1, tiled=True)]
    dot_general x5 -> x0, matrix products: 19.9 us -> none  [the longest x1 13.1 us: cycle_block(): jnp.einsum('sak,skb->sab', left, right, preferred_element_type=jnp.float32)]
    transpose x1 -> x0, local copies, waits for them, and re-layouts: 16 us -> none  [cycle_block(): left = left.reshape(slots, ROWCAP, TILE, TILE).transpose(0, 2, 1, 3).resh...]
  transfers between devices with their start and end apart: 3 -> 0, of which waited for: 2 -> 0; matrix products, arithmetic and copies ran while one was open for 18% -> 0% of each run, Pallas kernels for 0% -> 0%
where the time goes in v1:
time: 199 us
  Pallas kernels  184 us (92%)
  local copies, waits for them, and re-layouts  10.2 us (5%)
  other arithmetic  4.45 us (2%)
    pallas_call x1, Pallas kernels, local(): pl.pallas_call(kernel, out_shape=(jax.ShapeDtypeStruct((jdev, capt, area)...  184 us
    unnamed x10, local copies, waits for them, and re-layouts  4.02 us

profile of v1, /device:TPU:1, one launch (start us, length us, event | category | flops | bytes accessed | tf_op | source)
XLA Modules:
  0.0 199.0 jit_solution(5688143755336701931)
XLA Ops:
  0.6 0.0 copy-start
  0.7 0.7 compare_select_fusion.2
  1.3 0.7 broadcast_remainder_fusion
  2.0 0.6 fusion.12
  2.6 0.1 rem.86
  2.7 0.6 add_minimum_fusion
  3.4 0.1 pad_add_fusion.1.slot_of
  3.5 0.1 div.36
  3.6 0.1 ne.151
  3.7 0.0 copy-done
  3.7 0.7 gather_fusion
  4.3 0.6 dynamic_slice.18
  4.9 0.7 dynamic-slice_add_fusion
  5.7 0.1 broadcast_in_dim.92
  5.7 0.8 constant_dynamic-slice_fusion.1
  6.6 0.1 add.247.pair_e
  6.7 0.9 constant_dynamic-slice_fusion.2
  7.6 0.8 reshape.342
  8.3 0.6 gather_fusion.2
  8.9 0.6 gather_fusion.1
  9.5 0.1 convert_reduce_fusion
  9.6 0.1 add_select_fusion
  9.7 0.1 eq.63
  9.8 0.1 sub.25
  9.9 0.3 select_reduce_fusion
  10.2 0.2 select_reduce_fusion.4
  10.4 0.1 select_reduce_fusion.3
  10.6 0.1 fusion
  10.7 0.1 reshape.371.live
  10.7 0.0 copy-start.1
  10.7 1.4 copy-done.1
  12.2 0.0 copy-start.2
  12.2 0.9 copy-done.2
  13.1 0.0 copy-start.3
  13.1 0.9 copy-done.3
  14.1 183.6 %shard_map.95 = (bf16[2,16,4096]{2,1,0:T(8,128)(2,1)S(1)}, f32[8,128]{1,0:T(8,128)S(1)}) custom-call(s32[2,16,24]{2,1,0:T(8,128)S(1)} %pad_add_fusion.jobs, s32[32]{0:T(128)S(1)} %pad_add_fusion.1.slot_of, bf16[2,16,4096]{2,1,0:T(8,128)(2,1)S(1)} %bitcast.58, f32[32,1]{1,0:T(8,128)S(1)} %reshape.371.live, f32[32,1]{1,0:T(8,128)S(1)} %add.247.pair_e, ...), custom_call_target="tpu_custom_call" | custom-call | tf_op jit(solution)/shard_map/pallas_call | solution.py:341
  197.6 0.6 slice_reduce_fusion
  198.3 0.7 copy.33
  (14 shorter events, 0.1 us)
Async XLA Ops:
  0.6 3.0 %copy-start = (f32[200]{0:T(256)S(1)}, f32[200]{0:T(256)}, u32[]{:S(2)}) copy-start(f32[200]{0:T(256)} %param.14) | copy-start | bytes 2404
  10.7 1.4 copy-start.1
  12.2 0.9 copy-start.2
  13.1 0.9 copy-start.3

commit v2 on v1

--- a/solution.py
+++ b/solution.py
@@ -14,6 +14,9 @@
 NR = 8
 CAPT = 16
 NH = 6
+SIDE = 4
+QROWS = CAPT // SIDE * HALF
+HROWS = LIVE2 // 2 * HALF
 F32, BF16 = jnp.float32, jnp.bfloat16
 
 
@@ -24,15 +27,25 @@
 def kernel(
     jobs, slot_of, amps, live, pair_e, row_e, col_e, ovov_hbm, ints_hbm, hist_hbm,
     new_amps, gram,
-    ints, ovov, hist, stage, a_out, a_land, a_exp, mask, parts, c_land, total, cyc, g_one, g_two,
-    w_sem, in_sem, a_send, a_recv, c_send, c_recv, g_send, g_recv,
+    ints, ovov, hist, stage, a_out, z_land, a_land, a_exp, mask, parts, x_land, y_land, x_sum, y_sum,
+    x_last, y_last, total, cyc, g_one, g_two,
+    w_sem, in_sem, zs_send, zs_recv, xy_send, xy_recv, zg_send, zg_recv, fw_send, fw_recv,
+    x_send, x_recv, y_send, y_recv, xl_send, xl_recv, yl_send, yl_recv, g_send, g_recv,
 ):
     r = lax.axis_index("reorder")
     p = lax.axis_index("pair")
+    z, core = r // 2, r % 2
+    x, y = p % SIDE, p // SIDE
+    main = (p // 2) % 2 == core
     barrier = pltpu.get_barrier_semaphore()
 
-    def signal(device):
-        pl.semaphore_signal(barrier, inc=1, device_id=device, device_id_type=MESH)
+    def remote(src, dst, send, recv, device):
+        return pltpu.make_async_remote_copy(
+            src_ref=src, dst_ref=dst, send_sem=send, recv_sem=recv, device_id=device, device_id_type=MESH
+        )
+
+    def arrive(ref, sem):
+        pltpu.make_async_copy(ref, ref, sem).wait()
 
     w_copy = pltpu.make_async_copy(ints_hbm, ints, w_sem.at[0])
     w_copy.start()
@@ -41,67 +54,101 @@
     hist_copy = pltpu.make_async_copy(hist_hbm, hist, in_sem.at[1])
     hist_copy.start()
 
-    def greet_row(d, c):
-        signal(((r + d) % NR, p))
-        return c
-
-    def greet_pair(d, c):
-        signal((r, (p + d) % NP))
-        return c
-
-    own = p // 2 == r
-
-    def greet_amps(i, c):
-        @pl.when(jnp.logical_not(jnp.logical_and(own, i == p)))
-        def _():
-            signal((p // 2, i))
-
-        return c
-
-    lax.fori_loop(1, NR, greet_row, 0)
-    lax.fori_loop(1, NP, greet_pair, 0)
-    lax.fori_loop(0, NP, greet_amps, 0)
+    def greet(device):
+        pl.semaphore_signal(barrier, inc=1, device_id=device, device_id_type=MESH)
+
+    for d in range(1, NR):
+        greet(((r + d) % NR, p))
+    for d in range(1, NP):
+        greet((r, (p + d) % NP))
 
     lane_in, lane_out = iota((128, 128), 0), iota((128, 128), 1)
     half, q = lane_in // TILE, lane_in % TILE
     order = (lane_out == half * TILE + (q % 2) * HALF + q // 2).astype(BF16)
 
     def turn(m, c):
-        x = amps[:, :, pl.ds(pl.multiple_of(m * 128, 128), 128)].reshape(2 * CAPT, 128)
-        y = jnp.dot(x, order, preferred_element_type=F32)
-        stage[pl.ds(m, 2 * CAPT, stride=HALF), :] = y
+        v = amps[:, :, pl.ds(pl.multiple_of(m * 128, 128), 128)].reshape(2 * CAPT, 128)
+        w = jnp.dot(v, order, preferred_element_type=F32)
+        stage[pl.ds(m, 2 * CAPT, stride=HALF), :] = w
         return c
 
-    lax.fori_loop(0, HALF, turn, 0)
-    a_out[...] = stage[...].astype(BF16).reshape(2, CAPT * HALF, 128)
-
-    pl.semaphore_wait(barrier, NR - 1 + NP - 1 + 2 * NR - own.astype(jnp.int32))
-
-    def amps_copy(kk, d):
-        return pltpu.make_async_remote_copy(
-            src_ref=a_out.at[kk],
-            dst_ref=a_land.at[p],
-            send_sem=a_send.at[kk * NR + d],
-            recv_sem=a_recv.at[p],
-            device_id=((r + d) % NR, 2 * r + kk),
-            device_id_type=MESH,
-        )
-
-    def to_other(kk, d):
-        return jnp.logical_not(jnp.logical_and(d == 0, 2 * r + kk == p))
-
-    def send_amps(n, c):
-        @pl.when(to_other(n % 2, n // 2))
-        def _():
-            amps_copy(n % 2, n // 2).start()
-
-        return c
-
-    lax.fori_loop(0, 2 * NR, send_amps, 0)
-
-    @pl.when(own)
+    lax.fori_loop(0, HALF, turn, 0, unroll=8)
+    for quarter in range(SIDE):
+        for kk in range(2):
+            at = (kk * CAPT + quarter * CAPT // SIDE) * HALF
+            a_out[quarter, kk] = stage[at : at + QROWS].astype(BF16)
+
+    pl.semaphore_wait(barrier, NR - 1 + NP - 1)
+
+    def scatter(d):
+        to = (z + d) % SIDE
+        return remote(
+            a_out.at[to], z_land.at[z], zs_send.at[d - 1], zs_recv.at[z], (2 * to + core, p)
+        )
+
+    for d in range(1, SIDE):
+        scatter(d).start()
+    z_land[z] = a_out[z]
+
+    def turned(d, kk):
+        frm = (z + d) % SIDE
+        k = 4 * frm + 2 * core + kk
+        return frm, k, remote(
+            z_land.at[frm, kk], a_land.at[p, z], xy_send.at[2 * d + kk], xy_recv.at[p], (r, k)
+        )
+
+    for d in range(SIDE):
+        frm = (z + d) % SIDE
+        if d:
+            arrive(z_land.at[frm], zs_recv.at[frm])
+        for kk in range(2):
+            frm, k, copy = turned(d, kk)
+
+            @pl.when(k != p)
+            def _():
+                copy.start()
+
+            @pl.when(k == p)
+            def _():
+                a_land[p, z] = z_land[frm, kk]
+
+    def place_of(n):
+        d = (n + 1) % NP
+        return ((y + d // SIDE) % SIDE) * SIDE + (x + d % SIDE) % SIDE
+
+    def gather(i, e):
+        return remote(
+            a_land.at[i, z], a_land.at[i, z], zg_send.at[i, e - 1], zg_recv.at[i, z],
+            (2 * ((z + e) % SIDE) + core, p),
+        )
+
+    @pl.when(main)
     def _():
-        a_land[p] = a_out[p % 2]
+        def step(n, c):
+            i = place_of(n)
+
+            @pl.when(i != p)
+            def _():
+                arrive(a_land.at[i, z], xy_recv.at[i])
+
+            for e in range(1, SIDE):
+                gather(i, e).start()
+            return c
+
+        lax.fori_loop(0, NP, step, 0)
+
+    def forward(i):
+        return remote(a_land.at[i], a_land.at[i], fw_send.at[i], fw_recv.at[i], (r + 1 - 2 * core, p))
+
+    def collect(n):
+        i = place_of(n)
+
+        @pl.when(main)
+        def _():
+            for e in range(1, SIDE):
+                k = (z + e) % SIDE
+                arrive(a_land.at[i, k], zg_recv.at[i, k])
+            forward(i).start()
 
     lane_in, lane_out = iota((128, 256), 0), iota((128, 256), 1)
     spread = (lane_in == lane_out // 2).astype(BF16)
@@ -109,31 +156,78 @@
     mask[0] = (lane % 2 == 0).astype(BF16)
     mask[1] = (lane % 2 == 1).astype(BF16)
     mask[2] = jnp.zeros((CAPT, 128), BF16)
-    low = iota((1, 128), 1) < TILE
     low_f = (iota((TILE, 128), 1) < TILE).astype(F32)
     keep = (low_f.astype(BF16), (1.0 - low_f).astype(BF16))
     low = iota((HALF, 128), 1) < TILE
 
     w_copy.wait()
 
-    def parts_copy(i):
-        return pltpu.make_async_remote_copy(
-            src_ref=parts.at[i],
-            dst_ref=c_land.at[p],
-            send_sem=c_send.at[i],
-            recv_sem=c_recv.at[p],
-            device_id=(r, i),
-            device_id_type=MESH,
-        )
+    def x_copy(i):
+        xi, yi = i % SIDE, i // SIDE
+        return remote(
+            parts.at[i, pl.ds(0, HROWS)], x_land.at[x, yi], x_send.at[i], x_recv.at[x, yi],
+            (r, y * SIDE + xi),
+        )
+
+    def y_copy(i):
+        xi, yi = i % SIDE, i // SIDE
+        return remote(
+            parts.at[i, pl.ds(HROWS, HROWS)], y_land.at[y, xi], y_send.at[i], y_recv.at[y, xi],
+            (r, yi * SIDE + x),
+        )
+
+    def x_total(yi):
+        acc = parts[yi * SIDE + x, :HROWS].astype(F32)
+        for e in range(1, SIDE):
+            k = (x + e) % SIDE
+            arrive(x_land.at[k, yi], x_recv.at[k, yi])
+            acc += x_land[k, yi].astype(F32)
+        return acc
+
+    def y_total(xi):
+        acc = parts[y * SIDE + xi, HROWS:].astype(F32)
+        for e in range(1, SIDE):
+            k = (y + e) % SIDE
+            arrive(y_land.at[k, xi], y_recv.at[k, xi])
+            acc += y_land[k, xi].astype(F32)
+        return acc
+
+    def x_last_copy(e):
+        to = (y + e) % SIDE
+        return remote(
+            x_sum.at[e - 1], x_last.at[y], xl_send.at[e - 1], xl_recv.at[y], (r, to * SIDE + x)
+        )
+
+    def y_last_copy(e):
+        to = (x + e) % SIDE
+        return remote(
+            y_sum.at[e - 1], y_last.at[x], yl_send.at[e - 1], yl_recv.at[x], (r, y * SIDE + to)
+        )
+
+    def x_pass(e):
+        x_sum[e - 1] = x_total((y + e) % SIDE).astype(BF16)
+        x_last_copy(e).start()
+
+    def y_pass(e):
+        y_sum[e - 1] = y_total((x + e) % SIDE).astype(BF16)
+        y_last_copy(e).start()
+
+    collect(0)
 
     def one_first(n, c):
-        i = (p + 1 + n) % NP
-
-        @pl.when(jnp.logical_not(jnp.logical_and(own, i == p)))
-        def _():
-            pltpu.make_async_copy(a_land.at[i], a_land.at[i], a_recv.at[i]).wait()
-
-        wide = jnp.dot(a_land[i], spread, preferred_element_type=F32).astype(BF16)
+        i = place_of(n)
+
+        @pl.when(n < NP - 1)
+        def _():
+            collect(n + 1)
+
+        @pl.when(jnp.logical_not(main))
+        def _():
+            arrive(a_land.at[i], fw_recv.at[i])
+
+        wide = jnp.dot(
+            a_land[i].reshape(CAPT * HALF, 128), spread, preferred_element_type=F32
+        ).astype(BF16)
         a_exp[:, :HALF, :] = wide[:, :128].reshape(CAPT, HALF, 128)
         a_exp[:, HALF:, :] = wide[:, 128:].reshape(CAPT, HALF, 128)
 
@@ -142,8 +236,8 @@
             for side in range(2):
                 code = jobs[side, i, u]
                 tile, sel, at = code // 4 % CAPT, code % 4, code // (4 * CAPT)
-                x = a_exp[tile].reshape(4, CAPT, 128) * mask[sel][None]
-                rows.append(x.reshape(TILE, 128))
+                v = a_exp[tile].reshape(4, CAPT, 128) * mask[sel][None]
+                rows.append(v.reshape(TILE, 128))
                 w = ints[at]
                 cols += [w * keep[0], w * keep[1]]
             out = jnp.dot(
@@ -158,31 +252,47 @@
             parts[i, pl.ds(pl.multiple_of(u * HALF, HALF), HALF), :] = both.astype(BF16)
             return c
 
-        lax.fori_loop(0, LIVE2, job, 0, unroll=4)
-
-        @pl.when(i != p)
-        def _():
-            parts_copy(i).start()
+        lax.fori_loop(0, LIVE2, job, 0, unroll=LIVE2)
+
+        @pl.when(i % SIDE != x)
+        def _():
+            x_copy(i).start()
+
+        @pl.when(i // SIDE != y)
+        def _():
+            y_copy(i).start()
+
+        for e, after in ((1, 8), (2, 12)):
+
+            @pl.when(n == after)
+            def _(e=e):
+                x_pass(e)
 
         return c
 
     lax.fori_loop(0, NP, one_first, 0)
-
-    total[...] = parts[p].astype(F32).reshape(LIVE2, HALF, 128)
-
-    def add(d, c):
-        k = (p + NP - d) % NP
-        pltpu.make_async_copy(c_land.at[k], c_land.at[k], c_recv.at[k]).wait()
-        total[...] += c_land[k].astype(F32).reshape(LIVE2, HALF, 128)
-        return c
-
-    lax.fori_loop(1, NP, add, 0)
+    x_pass(3)
+    for e in range(1, SIDE):
+        y_pass(e)
+
+    top = x_total(y)
+    for e in range(1, SIDE):
+        k = (y + e) % SIDE
+        arrive(x_last.at[k], xl_recv.at[k])
+        top += x_last[k].astype(F32)
+    total[: LIVE2 // 2] = top.reshape(LIVE2 // 2, HALF, 128)
+    top = y_total(x)
+    for e in range(1, SIDE):
+        k = (x + e) % SIDE
+        arrive(y_last.at[k], yl_recv.at[k])
+        top += y_last[k].astype(F32)
+    total[LIVE2 // 2 :] = top.reshape(LIVE2 // 2, HALF, 128)
 
     def place(s, c):
         cyc[pl.ds(pl.multiple_of(s * HALF, HALF), HALF), :] = total[slot_of[s]]
         return c
 
-    lax.fori_loop(0, 2 * CAPT, place, 0)
+    lax.fori_loop(0, 2 * CAPT, place, 0, unroll=8)
     ovov_copy.wait()
     hist_copy.wait()
 
@@ -216,70 +326,65 @@
         mine = jnp.where(at_row == h, jnp.sum(s, axis=0, keepdims=True), mine)
 
     def row_copy(d):
-        return pltpu.make_async_remote_copy(
-            src_ref=g_one.at[r], dst_ref=g_one.at[r], send_sem=g_send.at[d],
-            recv_sem=g_recv.at[r], device_id=((r + d) % NR, p), device_id_type=MESH,
+        return remote(
+            g_one.at[r], g_one.at[r], g_send.at[d], g_recv.at[r], ((r + d) % NR, p)
         )
 
     def pair_copy(d):
-        return pltpu.make_async_remote_copy(
-            src_ref=g_two.at[p], dst_ref=g_two.at[p], send_sem=g_send.at[NR + d],
-            recv_sem=g_recv.at[NR + p], device_id=(r, (p + d) % NP), device_id_type=MESH,
-        )
-
-    def start_all(copy):
-        def step(d, c):
-            copy(d).start()
-            return c
-
-        return step
-
-    def sent_all(copy):
-        def step(d, c):
-            copy(d).wait_send()
-            return c
-
-        return step
+        return remote(
+            g_two.at[p], g_two.at[p], g_send.at[NR + d], g_recv.at[NR + p], (r, (p + d) % NP)
+        )
 
     g_one[r] = mine
-    lax.fori_loop(1, NR, start_all(row_copy), 0)
-
-    def got_row(d, c):
-        k = (r + NR - d) % NR
-        pltpu.make_async_copy(g_one.at[k], g_one.at[k], g_recv.at[k]).wait()
-        return c
-
-    lax.fori_loop(1, NR, got_row, 0)
+    for d in range(1, NR):
+        row_copy(d).start()
+    for d in range(1, NR):
+        k = (r + d) % NR
+        arrive(g_one.at[k], g_recv.at[k])
     g_two[p] = jnp.sum(g_one[...], axis=0)
-    lax.fori_loop(1, NP, start_all(pair_copy), 0)
-
-    def got_pair(d, c):
-        k = (p + NP - d) % NP
-        pltpu.make_async_copy(g_two.at[k], g_two.at[k], g_recv.at[NR + k]).wait()
-        return c
-
-    lax.fori_loop(1, NP, got_pair, 0)
+    for d in range(1, NP):
+        pair_copy(d).start()
+    for d in range(1, NP):
+        k = (p + d) % NP
+        arrive(g_two.at[k], g_recv.at[NR + k])
     everyone = jnp.sum(jnp.sum(g_two[...], axis=0), axis=1, keepdims=True)
     everyone = jnp.broadcast_to(everyone, (8, 128))
     gram[...] = jnp.where(at_row == NH, jnp.sqrt(everyone), everyone) / (TILE * NP)
 
-    lax.fori_loop(1, NR, sent_all(row_copy), 0)
-    lax.fori_loop(1, NP, sent_all(pair_copy), 0)
-
-    def sent_parts(d, c):
-        parts_copy((p + d) % NP).wait_send()
+    for d in range(1, NR):
+        row_copy(d).wait_send()
+    for d in range(1, NP):
+        pair_copy(d).wait_send()
+    for d in range(1, SIDE):
+        scatter(d).wait_send()
+        x_last_copy(d).wait_send()
+        y_last_copy(d).wait_send()
+    for d in range(SIDE):
+        for kk in range(2):
+            frm, k, copy = turned(d, kk)
+
+            @pl.when(k != p)
+            def _():
+                copy.wait_send()
+
+    def sent(i, c):
+        @pl.when(i % SIDE != x)
+        def _():
+            x_copy(i).wait_send()
+
+        @pl.when(i // SIDE != y)
+        def _():
+            y_copy(i).wait_send()
+
+        @pl.when(main)
+        def _():
+            for e in range(1, SIDE):
+                gather(i, e).wait_send()
+            forward(i).wait_send()
+
         return c
 
-    lax.fori_loop(1, NP, sent_parts, 0)
-
-    def sent_amps(n, c):
-        @pl.when(to_other(n % 2, n // 2))
-        def _():
-            amps_copy(n % 2, n // 2).wait_send()
-
-        return c
-
-    lax.fori_loop(0, 2 * NR, sent_amps, 0)
+    lax.fori_loop(0, NP, sent, 0)
 
 
 def tables(tile_index, first, second, across):
@@ -351,22 +456,40 @@
             pltpu.VMEM((jdev, capt, area), BF16),
             pltpu.VMEM((NH, jdev, capt, area), BF16),
             pltpu.VMEM((2 * capt * HALF, 128), F32),
-            pltpu.VMEM((2, capt * HALF, 128), BF16),
-            pltpu.VMEM((NP, capt * HALF, 128), BF16),
+            pltpu.VMEM((SIDE, 2, QROWS, 128), BF16),
+            pltpu.VMEM((SIDE, 2, QROWS, 128), BF16),
+            pltpu.VMEM((NP, SIDE, QROWS, 128), BF16),
             pltpu.VMEM((capt, TILE, 128), BF16),
             pltpu.VMEM((3, capt, 128), BF16),
             pltpu.VMEM((NP, LIVE2 * HALF, 128), BF16),
-            pltpu.VMEM((NP, LIVE2 * HALF, 128), BF16),
+            pltpu.VMEM((SIDE, SIDE, HROWS, 128), BF16),
+            pltpu.VMEM((SIDE, SIDE, HROWS, 128), BF16),
+            pltpu.VMEM((SIDE - 1, HROWS, 128), BF16),
+            pltpu.VMEM((SIDE - 1, HROWS, 128), BF16),
+            pltpu.VMEM((SIDE, HROWS, 128), BF16),
+            pltpu.VMEM((SIDE, HROWS, 128), BF16),
             pltpu.VMEM((LIVE2, HALF, 128), F32),
             pltpu.VMEM((2 * capt * HALF, 128), F32),
             pltpu.VMEM((NR, 8, 128), F32),
             pltpu.VMEM((NP, 8, 128), F32),
             dma((1,)),
             dma((2,)),
-            dma((2 * NR,)),
+            dma((SIDE - 1,)),
+            dma((SIDE,)),
+            dma((NR,)),
+            dma((NP,)),
+            dma((NP, SIDE - 1)),
+            dma((NP, SIDE)),
             dma((NP,)),
             dma((NP,)),
             dma((NP,)),
+            dma((SIDE, SIDE)),
+            dma((NP,)),
+            dma((SIDE, SIDE)),
+            dma((SIDE - 1,)),
+            dma((SIDE,)),
+            dma((SIDE - 1,)),
+            dma((SIDE,)),
             dma((NR + NP,)),
             dma((NR + NP,)),
         ],

time: 199 us -> 91.7 us (0.46)
  Pallas kernels: 184 us -> 75.9 us
    pallas_call x1, Pallas kernels: 184 us -> 75.9 us  [local(): pl.pallas_call(kernel, out_shape=(jax.ShapeDtypeStruct((jdev, capt, area)...]
where the time goes in v2:
time: 91.7 us; the launch traced here: 91.3 us
  Pallas kernels  75.9 us (83%)
  local copies, waits for them, and re-layouts  10.2 us (11%)
  other arithmetic  4.45 us (5%)
    pallas_call x1, Pallas kernels, local(): pl.pallas_call(kernel, out_shape=(jax.ShapeDtypeStruct((jdev, capt, area)...  75.9 us
    unnamed x10, local copies, waits for them, and re-layouts  4.02 us

profile of v2, /device:TPU:1, one launch (start us, length us, event | category | flops | bytes accessed | tf_op | source)
XLA Modules:
  0.0 91.3 jit_solution(3006055982753043460)
XLA Ops:
  0.6 0.0 copy-start
  0.7 0.7 compare_select_fusion.2
  1.3 0.7 broadcast_remainder_fusion
  2.0 0.6 fusion.12
  2.6 0.1 rem.86
  2.7 0.6 add_minimum_fusion
  3.4 0.1 pad_add_fusion.1.slot_of
  3.5 0.1 div.36
  3.6 0.1 ne.151
  3.7 0.0 copy-done
  3.7 0.7 gather_fusion
  4.3 0.6 dynamic_slice.18
  4.9 0.7 dynamic-slice_add_fusion
  5.7 0.1 broadcast_in_dim.92
  5.7 0.8 constant_dynamic-slice_fusion.1
  6.6 0.1 add.247.pair_e
  6.7 0.9 constant_dynamic-slice_fusion.2
  7.6 0.8 reshape.342
  8.3 0.6 gather_fusion.2
  8.9 0.6 gather_fusion.1
  9.5 0.1 convert_reduce_fusion
  9.6 0.1 add_select_fusion
  9.7 0.1 eq.63
  9.8 0.1 sub.25
  9.9 0.3 select_reduce_fusion
  10.2 0.2 select_reduce_fusion.4
  10.4 0.1 select_reduce_fusion.3
  10.6 0.1 fusion
  10.7 0.1 reshape.371.live
  10.7 0.0 copy-start.1
  10.7 1.4 %copy-done.1 = bf16[6,1,2,16,4096]{4,3,2,1,0:T(8,128)(2,1)S(1)} copy-done((bf16[6,1,2,16,4096]{4,3,2,1,0:T(8,128)(2,1)S(1)}, bf16[6,1,2,16,4096]{4,3,2,1,0:T(8,128)(2,1)}, u32[]{:S(2)}) %copy-start.1) | copy-done | bytes 1572888
  12.2 0.0 copy-start.2
  12.2 0.9 %copy-done.2 = bf16[1,2,16,4096]{3,2,1,0:T(8,128)(2,1)S(1)} copy-done((bf16[1,2,16,4096]{3,2,1,0:T(8,128)(2,1)S(1)}, bf16[1,2,16,4096]{3,2,1,0:T(8,128)(2,1)}, u32[]{:S(2)}) %copy-start.2) | copy-done | bytes 262168
  13.1 0.0 copy-start.3
  13.1 0.9 %copy-done.3 = bf16[1,2,16,4096]{3,2,1,0:T(8,128)(2,1)S(1)} copy-done((bf16[1,2,16,4096]{3,2,1,0:T(8,128)(2,1)S(1)}, bf16[1,2,16,4096]{3,2,1,0:T(8,128)(2,1)}, u32[]{:S(2)}) %copy-start.3) | copy-done | bytes 262168
  14.1 75.9 %shard_map.95 = (bf16[2,16,4096]{2,1,0:T(8,128)(2,1)S(1)}, f32[8,128]{1,0:T(8,128)S(1)}) custom-call(s32[2,16,24]{2,1,0:T(8,128)S(1)} %pad_add_fusion.jobs, s32[32]{0:T(128)S(1)} %pad_add_fusion.1.slot_of, bf16[2,16,4096]{2,1,0:T(8,128)(2,1)S(1)} %bitcast.58, f32[32,1]{1,0:T(8,128)S(1)} %reshape.371.live, f32[32,1]{1,0:T(8,128)S(1)} %add.247.pair_e, ...), custom_call_target="tpu_custom_call" | custom-call | tf_op jit(solution)/shard_map/pallas_call | solution.py:446
  89.9 0.6 slice_reduce_fusion
  90.6 0.7 copy.33
  (14 shorter events, 0.1 us)
Async XLA Ops:
  0.6 3.0 %copy-start = (f32[200]{0:T(256)S(1)}, f32[200]{0:T(256)}, u32[]{:S(2)}) copy-start(f32[200]{0:T(256)} %param.14) | copy-start | bytes 2404
  10.7 1.4 %copy-start.1 = (bf16[6,1,2,16,4096]{4,3,2,1,0:T(8,128)(2,1)S(1)}, bf16[6,1,2,16,4096]{4,3,2,1,0:T(8,128)(2,1)}, u32[]{:S(2)}) copy-start(bf16[6,1,2,16,4096]{4,3,2,1,0:T(8,128)(2,1)} %param.12) | copy-start | bytes 4718596
  12.2 0.9 %copy-start.2 = (bf16[1,2,16,4096]{3,2,1,0:T(8,128)(2,1)S(1)}, bf16[1,2,16,4096]{3,2,1,0:T(8,128)(2,1)}, u32[]{:S(2)}) copy-start(bf16[1,2,16,4096]{3,2,1,0:T(8,128)(2,1)} %param.8) | copy-start | bytes 786436
  13.1 0.9 %copy-start.3 = (bf16[1,2,16,4096]{3,2,1,0:T(8,128)(2,1)S(1)}, bf16[1,2,16,4096]{3,2,1,0:T(8,128)(2,1)}, u32[]{:S(2)}) copy-start(bf16[1,2,16,4096]{3,2,1,0:T(8,128)(2,1)} %param.10) | copy-start | bytes 786436

commit v3 on v2

--- a/solution.py
+++ b/solution.py
@@ -14,9 +14,15 @@
 NR = 8
 CAPT = 16
 NH = 6
+NT = 25
+DEAD = NT * NT
 SIDE = 4
 QROWS = CAPT // SIDE * HALF
 HROWS = LIVE2 // 2 * HALF
+ORDER = (
+    (2, 2), (2, 1), (1, 2), (2, 3), (3, 2), (1, 1), (3, 1), (1, 3), (3, 3),
+    (2, 0), (0, 2), (1, 0), (0, 1), (3, 0), (0, 3), (0, 0),
+)
 F32, BF16 = jnp.float32, jnp.bfloat16
 
 
@@ -24,12 +30,103 @@
     return lax.broadcasted_iota(jnp.int32, shape, dim)
 
 
+def column(row):
+    eye = iota((CAPT, CAPT), 0) == iota((CAPT, CAPT), 1)
+    return jnp.sum(jnp.where(eye, row, 0), axis=1, keepdims=True)
+
+
+def row_col(tile):
+    row = (tile * 5243) >> 17
+    return row, tile - NT * row
+
+
+def tables(p, r, tiles, codes):
+    t = iota((CAPT, 1), 0)
+    u = iota((1, 128), 1)
+
+    def one(i, carry):
+        def get(j):
+            return column(tiles[i, pl.ds(j, 1), :])
+
+        inner, first, second = get(p), get(2 * r), get(2 * r + 1)
+        in_row, in_col = row_col(inner)
+        count = jnp.sum((first < DEAD).astype(jnp.int32), axis=0, keepdims=True)
+        place = jnp.where(first < DEAD, t, -1)
+        place_two = jnp.where(second < DEAD, t + count, -1)
+        packed = DEAD + jnp.sum(
+            jnp.where(place == u, first - DEAD, 0) + jnp.where(place_two == u, second - DEAD, 0),
+            axis=0,
+            keepdims=True,
+        )
+        out_row, out_col = row_col(packed)
+        same = jnp.logical_and(in_row == out_row, inner < DEAD)
+        lowest = jnp.min(jnp.where(same, t, CAPT), axis=0, keepdims=True)
+        highest = jnp.max(jnp.where(same, t, -1), axis=0, keepdims=True)
+        base = in_col * (NT * CAPT) + t
+        which = jnp.where(u < count, 0, 1)
+
+        def entry(pick, present):
+            found = jnp.sum(jnp.where(t == pick, base, 0), axis=0, keepdims=True)
+            found = (found + out_col * CAPT) * 4 + which
+            return jnp.where(present, found, 2)
+
+        codes[pl.ds(i, 1), :] = entry(lowest, lowest < CAPT)
+        codes[pl.ds(NP + i, 1), :] = entry(highest, highest > lowest)
+        return carry
+
+    lax.fori_loop(0, NP, one, 0, unroll=4)
+    own = tiles[p, pl.ds(2 * r, 1), :]
+    count = jnp.sum((own < DEAD).astype(jnp.int32), axis=1, keepdims=True)
+    slot = jnp.where(u < CAPT, u, jnp.minimum(u - CAPT + count, LIVE2 - 1))
+    codes[2 * NP : 2 * NP + 8, :] = jnp.broadcast_to(slot, (8, 128))
+
+
+def denominators(p, r, tiles, vir, slab, eps_occ, inverse):
+    own = [column(tiles[p, pl.ds(2 * r + j, 1), :]) for j in range(2)]
+    tile = jnp.concatenate(own, axis=0)
+    alive = jnp.broadcast_to((tile < DEAD).astype(F32), (2 * CAPT, 128))
+    row, col = row_col(tile)
+    row = jnp.minimum(row, NT - 1)
+    lines = [vir[pl.ds(n * 128, 128)].reshape(1, 128) for n in range(NT // 2)]
+    last = vir[pl.ds(NT // 2 * 128, TILE)].reshape(1, TILE)
+    lines.append(jnp.concatenate([last, last], axis=1))
+    lines.append(jnp.zeros((CAPT - len(lines), 128), F32))
+    lines = jnp.concatenate(lines, axis=0)
+    lane = iota((2 * CAPT, 128), 1)
+
+    def energies(index):
+        pair = index >> 1
+        pick = (iota((2 * CAPT, CAPT), 1) == pair).astype(F32)
+        both = jnp.dot(pick, lines, precision=lax.Precision.HIGHEST, preferred_element_type=F32)
+        other = pltpu.roll(both, TILE, 1)
+        return jnp.where(lane // TILE == index - 2 * pair, both, other)
+
+    rows, cols = energies(row), energies(col)
+
+    def occ(j):
+        return eps_occ[jnp.clip(slab[j], 0, eps_occ.shape[0] - 1)]
+
+    first, second = occ(p), [occ(2 * r + j) for j in range(2)]
+    base = jnp.where(iota((2 * CAPT, 128), 0) < CAPT, first + second[0], first + second[1]) - cols
+    pick_q, pick_lane = iota((128, 128), 0), iota((128, 128), 1) // TILE
+
+    def one(m, c):
+        pick = (pick_q == 2 * m + pick_lane).astype(F32)
+        row = jnp.dot(rows, pick, precision=lax.Precision.HIGHEST, preferred_element_type=F32)
+        at = pl.ds(pl.multiple_of(m * 2 * CAPT, 2 * CAPT), 2 * CAPT)
+        inverse[at, :] = alive / (base - row)
+        return c
+
+    lax.fori_loop(0, HALF, one, 0, unroll=4)
+    return alive
+
+
 def kernel(
-    jobs, slot_of, amps, live, pair_e, row_e, col_e, ovov_hbm, ints_hbm, hist_hbm,
+    slab, eps_occ, amps_hbm, tiles_hbm, ovov_hbm, ints_hbm, hist_hbm, vir_hbm,
     new_amps, gram,
-    ints, ovov, hist, stage, a_out, z_land, a_land, a_exp, mask, parts, x_land, y_land, x_sum, y_sum,
+    amps, tiles, vir, codes, jobs, inverse, ints, ovov, hist, stage, a_out, z_land, a_land, a_exp, mask, parts, x_land, y_land, x_sum, y_sum,
     x_last, y_last, total, cyc, g_one, g_two,
-    w_sem, in_sem, zs_send, zs_recv, xy_send, xy_recv, zg_send, zg_recv, fw_send, fw_recv,
+    in_sem, code_sem, zs_send, zs_recv, xy_send, xy_recv, zg_send, zg_recv, fw_send, fw_recv,
     x_send, x_recv, y_send, y_recv, xl_send, xl_recv, yl_send, yl_recv, g_send, g_recv,
 ):
     r = lax.axis_index("reorder")
@@ -47,12 +144,15 @@
     def arrive(ref, sem):
         pltpu.make_async_copy(ref, ref, sem).wait()
 
-    w_copy = pltpu.make_async_copy(ints_hbm, ints, w_sem.at[0])
-    w_copy.start()
-    ovov_copy = pltpu.make_async_copy(ovov_hbm, ovov, in_sem.at[0])
-    ovov_copy.start()
-    hist_copy = pltpu.make_async_copy(hist_hbm, hist, in_sem.at[1])
-    hist_copy.start()
+    loads = [
+        pltpu.make_async_copy(src, dst, in_sem.at[n])
+        for n, (src, dst) in enumerate(
+            ((amps_hbm, amps), (tiles_hbm, tiles), (vir_hbm, vir), (ints_hbm, ints), (ovov_hbm, ovov), (hist_hbm, hist))
+        )
+    ]
+    for load in loads:
+        load.start()
+    amps_copy, tiles_copy, vir_copy, w_copy, ovov_copy, hist_copy = loads
 
     def greet(device):
         pl.semaphore_signal(barrier, inc=1, device_id=device, device_id_type=MESH)
@@ -72,6 +172,7 @@
         stage[pl.ds(m, 2 * CAPT, stride=HALF), :] = w
         return c
 
+    amps_copy.wait()
     lax.fori_loop(0, HALF, turn, 0, unroll=8)
     for quarter in range(SIDE):
         for kk in range(2):
@@ -89,6 +190,13 @@
     for d in range(1, SIDE):
         scatter(d).start()
     z_land[z] = a_out[z]
+
+    tiles_copy.wait()
+    vir_copy.wait()
+    tables(p, r, tiles, codes)
+    code_copy = pltpu.make_async_copy(codes, jobs, code_sem.at[0])
+    code_copy.start()
+    alive = denominators(p, r, tiles, vir, slab, eps_occ, inverse)
 
     def turned(d, kk):
         frm = (z + d) % SIDE
@@ -113,7 +221,9 @@
                 a_land[p, z] = z_land[frm, kk]
 
     def place_of(n):
-        d = (n + 1) % NP
+        d = 0
+        for at, (dx, dy) in enumerate(ORDER):
+            d = jnp.where(n == at, dy * SIDE + dx, d)
         return ((y + d // SIDE) % SIDE) * SIDE + (x + d % SIDE) % SIDE
 
     def gather(i, e):
@@ -161,6 +271,7 @@
     low = iota((HALF, 128), 1) < TILE
 
     w_copy.wait()
+    code_copy.wait()
 
     def x_copy(i):
         xi, yi = i % SIDE, i // SIDE
@@ -234,8 +345,9 @@
         def job(u, c):
             rows, cols = [], []
             for side in range(2):
-                code = jobs[side, i, u]
-                tile, sel, at = code // 4 % CAPT, code % 4, code // (4 * CAPT)
+                code = jobs[side * NP + i, u]
+                tile, sel, at = (code >> 2) & (CAPT - 1), code & 3, code >> 6
+                sel, at = jnp.minimum(sel, 2), jnp.clip(at, 0, DEAD - 1)
                 v = a_exp[tile].reshape(4, CAPT, 128) * mask[sel][None]
                 rows.append(v.reshape(TILE, 128))
                 w = ints[at]
@@ -262,18 +374,19 @@
         def _():
             y_copy(i).start()
 
-        for e, after in ((1, 8), (2, 12)):
-
-            @pl.when(n == after)
+        for e in range(1, SIDE):
+
+            @pl.when(n == ORDER.index((e, 0)))
+            def _(e=e):
+                y_pass(e)
+
+            @pl.when(n == ORDER.index((0, e)))
             def _(e=e):
                 x_pass(e)
 
         return c
 
     lax.fori_loop(0, NP, one_first, 0)
-    x_pass(3)
-    for e in range(1, SIDE):
-        y_pass(e)
 
     top = x_total(y)
     for e in range(1, SIDE):
@@ -289,29 +402,19 @@
     total[LIVE2 // 2 :] = top.reshape(LIVE2 // 2, HALF, 128)
 
     def place(s, c):
-        cyc[pl.ds(pl.multiple_of(s * HALF, HALF), HALF), :] = total[slot_of[s]]
+        cyc[pl.ds(pl.multiple_of(s * HALF, HALF), HALF), :] = total[jnp.clip(jobs[2 * NP, s], 0, LIVE2 - 1)]
         return c
 
     lax.fori_loop(0, 2 * CAPT, place, 0, unroll=8)
     ovov_copy.wait()
     hist_copy.wait()
 
-    alive = jnp.broadcast_to(live[...], (2 * CAPT, 128))
-    col = jnp.concatenate([col_e[...], col_e[...]], axis=1)
-    base = pair_e[...] - col
-    rows = row_e[...]
-    pick_q, pick_lane = iota((TILE, 128), 0), iota((TILE, 128), 1) // TILE
-
-    def finish(m, sums):
+    def correlate(m, sums):
         at = pl.ds(pl.multiple_of(m * 128, 128), 128)
         cycle = cyc[pl.ds(m, 2 * CAPT, stride=HALF), :]
         ov = ovov[:, :, at].reshape(2 * CAPT, 128).astype(F32)
         resid = (ov + cycle) * alive
-        pick = (pick_q == 2 * m + pick_lane).astype(F32)
-        row = jnp.dot(rows, pick, precision=lax.Precision.HIGHEST, preferred_element_type=F32)
-        old = amps[:, :, at].reshape(2 * CAPT, 128).astype(F32)
-        new = (old + resid / (base - row)) * alive
-        new_amps[:, :, at] = new.astype(BF16).reshape(2, CAPT, 128)
+        stage[pl.ds(pl.multiple_of(m * 2 * CAPT, 2 * CAPT), 2 * CAPT), :] = resid
         terms = [hist[h, :, :, at].reshape(2 * CAPT, 128).astype(F32) for h in range(NH)]
         terms.append(resid)
         return tuple(
@@ -319,7 +422,7 @@
         )
 
     zero = jnp.zeros((8, 128), F32)
-    sums = lax.fori_loop(0, HALF, finish, (zero,) * (NH + 1))
+    sums = lax.fori_loop(0, HALF, correlate, (zero,) * (NH + 1), unroll=4)
     at_row = iota((8, 128), 0)
     mine = zero
     for h, s in enumerate(sums):
@@ -338,6 +441,16 @@
     g_one[r] = mine
     for d in range(1, NR):
         row_copy(d).start()
+
+    def update(m, c):
+        at = pl.ds(pl.multiple_of(m * 128, 128), 128)
+        rows = pl.ds(pl.multiple_of(m * 2 * CAPT, 2 * CAPT), 2 * CAPT)
+        old = amps[:, :, at].reshape(2 * CAPT, 128).astype(F32)
+        new = old * alive + stage[rows, :] * inverse[rows, :]
+        new_amps[:, :, at] = new.astype(BF16).reshape(2, CAPT, 128)
+        return c
+
+    lax.fori_loop(0, HALF, update, 0, unroll=8)
     for d in range(1, NR):
         k = (r + d) % NR
         arrive(g_one.at[k], g_recv.at[k])
@@ -387,61 +500,16 @@
     lax.fori_loop(0, NP, sent, 0)
 
 
-def tables(tile_index, first, second, across):
-    dead = across * across
-    ns, _, capt = tile_index.shape
-    t = jnp.arange(capt, dtype=jnp.int32)
-    inner = lax.dynamic_slice(tile_index, (0, first, 0), (ns, 1, capt))
-    outer = lax.dynamic_slice(tile_index, (0, second, 0), (ns, 2, capt))
-    count = jnp.sum((outer[:, :1] < dead).astype(jnp.int32), axis=2, keepdims=True)
-    shift = jnp.concatenate([jnp.zeros_like(count), count], axis=1)
-    place = jnp.where(outer < dead, t + shift, -1).reshape(ns, 1, 2 * capt)
-    u = jnp.arange(LIVE2, dtype=jnp.int32)[None, :, None]
-    packed = jnp.sum(
-        jnp.where(place == u, outer.reshape(ns, 1, 2 * capt) - dead, 0), axis=2, keepdims=True
-    ) + dead
-    which = (u >= count).astype(jnp.int32)
-    same = (packed // across == inner // across) & (inner < dead)
-    none = dead * capt
-    code = (inner % across) * across * capt + t
-    lowest = jnp.min(jnp.where(same, t, capt), axis=2, keepdims=True)
-    highest = jnp.max(jnp.where(same, t, -1), axis=2, keepdims=True)
-
-    def entry(pick, present):
-        found = jnp.sum(jnp.where(t == pick, code, 0), axis=2, keepdims=True)
-        found = found + (packed % across) * capt
-        return jnp.where(present, found * 4 + which, 2)[..., 0]
-
-    jobs = jnp.stack([entry(lowest, lowest < capt), entry(highest, highest > lowest)])
-    return jobs
-
-
 def local(amps, tile_index, ovov, cycle_ints, history, slab, eps_occ, eps_vir):
     _, jdev, capt, area = amps.shape
     across = cycle_ints.shape[2]
     dead = across * across
-    p = lax.axis_index("pair")
-    r = lax.axis_index("reorder")
-    jobs = tables(tile_index, p, r * jdev, across)
-    local_idx = lax.dynamic_slice(tile_index, (p, r * jdev, 0), (1, jdev, capt))[0]
-    slots = jnp.arange(capt, dtype=jnp.int32)
-    count = jnp.sum((local_idx[0] < dead).astype(jnp.int32))
-    slot_of = jnp.concatenate([slots, jnp.minimum(slots + count, LIVE2 - 1)])
-    flat = local_idx.reshape(-1)
-    live = (flat < dead).astype(F32)[:, None]
-    occ = eps_occ[slab]
-    pair_e = lax.dynamic_slice(occ, (p,), (1,)) + jnp.repeat(
-        lax.dynamic_slice(occ, (r * jdev,), (jdev,)), capt
-    )
-    vir = eps_vir.reshape(across, TILE)
-    row_e = vir[jnp.minimum(flat // across, across - 1)]
-    col_e = vir[flat % across]
     ints = cycle_ints[0].transpose(1, 2, 0, 3).reshape(dead, 2, HALF, 128)
     ints = ints.transpose(0, 2, 1, 3).reshape(dead, TILE, 128)
 
     vmem = pl.BlockSpec(memory_space=pltpu.VMEM)
     smem = pl.BlockSpec(memory_space=pltpu.SMEM)
-    hbm = pl.BlockSpec(memory_space=pl.ANY)
+    hbm = pl.BlockSpec(memory_space=pltpu.HBM)
     dma = pltpu.SemaphoreType.DMA
     new_amps, gram = pl.pallas_call(
         kernel,
@@ -449,9 +517,15 @@
             jax.ShapeDtypeStruct((jdev, capt, area), BF16),
             jax.ShapeDtypeStruct((8, 128), F32),
         ),
-        in_specs=[smem, smem, vmem, vmem, vmem, vmem, vmem, hbm, hbm, hbm],
+        in_specs=[smem, smem] + [hbm] * 6,
         out_specs=(vmem, vmem),
         scratch_shapes=[
+            pltpu.VMEM((jdev, capt, area), BF16),
+            pltpu.VMEM(tile_index.shape, jnp.int32),
+            pltpu.VMEM(eps_vir.shape, F32),
+            pltpu.VMEM((2 * NP + 8, 128), jnp.int32),
+            pltpu.SMEM((2 * NP + 8, 128), jnp.int32),
+            pltpu.VMEM((2 * capt * HALF, 128), F32),
             pltpu.VMEM((dead, TILE, 128), BF16),
             pltpu.VMEM((jdev, capt, area), BF16),
             pltpu.VMEM((NH, jdev, capt, area), BF16),
@@ -472,8 +546,8 @@
             pltpu.VMEM((2 * capt * HALF, 128), F32),
             pltpu.VMEM((NR, 8, 128), F32),
             pltpu.VMEM((NP, 8, 128), F32),
+            dma((6,)),
             dma((1,)),
-            dma((2,)),
             dma((SIDE - 1,)),
             dma((SIDE,)),
             dma((NR,)),
@@ -496,7 +570,7 @@
         compiler_params=pltpu.CompilerParams(
             collective_id=0, has_side_effects=True, vmem_limit_bytes=48 << 20
         ),
-    )(jobs, slot_of, amps[0], live, pair_e[:, None], row_e, col_e, ovov[0], ints, history[:, 0])
+    )(slab, eps_occ, amps[0], tile_index, ovov[0], ints, history[:, 0], eps_vir)
     return new_amps[None], gram[: NH + 1, 0]
 
 

time: 91.7 us -> 70.8 us (0.77)
  Pallas kernels: 75.9 us -> 62.3 us
  other arithmetic: 4.45 us -> 0 us
  local copies, waits for them, and re-layouts: 10.2 us -> 7.56 us
    pallas_call x1, Pallas kernels: 75.9 us -> 62.3 us  [local(): pl.pallas_call(kernel, out_shape=(jax.ShapeDtypeStruct((jdev, capt, area)...]
    unnamed x10 -> x15, local copies, waits for them, and re-layouts: 4.02 us -> 6.94 us
    dynamic_slice x3 -> x0, local copies, waits for them, and re-layouts: 2.3 us -> none  [the longest x1 0.86 us: tables(): outer = lax.dynamic_slice(tile_index, (0, second, 0), (ns, 2, capt))]
    gather x3 -> x0, local copies, waits for them, and re-layouts: 1.81 us -> none  [the longest x1 0.66 us: local(): occ = eps_occ[slab]]
    reduce_sum x4 -> x0, other arithmetic: 1.22 us -> none  [the longest x1 0.63 us: local(): count = jnp.sum((local_idx[0] < dead).astype(jnp.int32))]
where the time goes in v3:
time: 70.8 us; the launch traced here: 70.6 us
  Pallas kernels  62.3 us (88%)
  local copies, waits for them, and re-layouts  7.56 us (11%)
    pallas_call x1, Pallas kernels, local(): pl.pallas_call(kernel, out_shape=(jax.ShapeDtypeStruct((jdev, capt, area)...  62.3 us
    unnamed x15, local copies, waits for them, and re-layouts  6.94 us

profile of v3, /device:TPU:1, one launch (start us, length us, event | category | flops | bytes accessed | tf_op | source)
XLA Modules:
  0.0 70.6 jit_solution(8953441886096172852)
XLA Ops:
  0.6 0.0 copy-start
  0.6 1.4 %copy-done = bf16[6,1,2,16,4096]{4,3,2,1,0:T(8,128)(2,1)S(1)} copy-done((bf16[6,1,2,16,4096]{4,3,2,1,0:T(8,128)(2,1)S(1)}, bf16[6,1,2,16,4096]{4,3,2,1,0:T(8,128)(2,1)}, u32[]{:S(2)}) %copy-start) | copy-done | bytes 1572888
  2.0 0.0 copy-start.1
  2.0 0.9 %copy-done.1 = bf16[1,2,16,4096]{3,2,1,0:T(8,128)(2,1)S(1)} copy-done((bf16[1,2,16,4096]{3,2,1,0:T(8,128)(2,1)S(1)}, bf16[1,2,16,4096]{3,2,1,0:T(8,128)(2,1)}, u32[]{:S(2)}) %copy-start.1) | copy-done | bytes 262168
  3.0 0.0 copy-start.2
  3.0 0.9 %copy-done.2 = bf16[1,2,16,4096]{3,2,1,0:T(8,128)(2,1)S(1)} copy-done((bf16[1,2,16,4096]{3,2,1,0:T(8,128)(2,1)S(1)}, bf16[1,2,16,4096]{3,2,1,0:T(8,128)(2,1)}, u32[]{:S(2)}) %copy-start.2) | copy-done | bytes 262168
  3.9 0.0 copy-start.3
  3.9 0.9 %copy-done.3 = s32[16,16,16]{2,1,0:T(8,128)S(1)} copy-done((s32[16,16,16]{2,1,0:T(8,128)S(1)}, s32[16,16,16]{2,1,0:T(8,128)}, u32[]{:S(2)}) %copy-start.3) | copy-done | bytes 16408
  4.8 0.0 copy-start.4
  4.8 0.7 copy-done.4
  5.5 0.0 copy-start.5
  5.5 0.7 copy-done.5
  6.2 0.0 copy-start.6
  6.2 0.7 copy-done.6
  6.9 62.3 %shard_map.95 = (bf16[2,16,4096]{2,1,0:T(8,128)(2,1)S(1)}, f32[8,128]{1,0:T(8,128)S(1)}) custom-call(s32[16]{0:T(128)S(1)} %copy-done.6, f32[200]{0:T(256)S(1)} %copy-done.5, bf16[2,16,4096]{2,1,0:T(8,128)(2,1)S(1)} %bitcast.14, s32[16,16,16]{2,1,0:T(8,128)S(1)} %copy-done.3, bf16[2,16,4096]{2,1,0:T(8,128)(2,1)S(1)} %bitcast.15, ...), custom_call_target="tpu_custom_call" | custom-call | tf_op jit(solution)/shard_map/pallas_call | solution.py:514
  69.2 0.6 slice_reduce_fusion
  69.9 0.7 copy.13
Async XLA Ops:
  0.6 1.4 %copy-start = (bf16[6,1,2,16,4096]{4,3,2,1,0:T(8,128)(2,1)S(1)}, bf16[6,1,2,16,4096]{4,3,2,1,0:T(8,128)(2,1)}, u32[]{:S(2)}) copy-start(bf16[6,1,2,16,4096]{4,3,2,1,0:T(8,128)(2,1)} %param.12) | copy-start | bytes 4718596
  2.0 0.9 %copy-start.1 = (bf16[1,2,16,4096]{3,2,1,0:T(8,128)(2,1)S(1)}, bf16[1,2,16,4096]{3,2,1,0:T(8,128)(2,1)}, u32[]{:S(2)}) copy-start(bf16[1,2,16,4096]{3,2,1,0:T(8,128)(2,1)} %param.8) | copy-start | bytes 786436
  3.0 0.9 %copy-start.2 = (bf16[1,2,16,4096]{3,2,1,0:T(8,128)(2,1)S(1)}, bf16[1,2,16,4096]{3,2,1,0:T(8,128)(2,1)}, u32[]{:S(2)}) copy-start(bf16[1,2,16,4096]{3,2,1,0:T(8,128)(2,1)} %param.10) | copy-start | bytes 786436
  3.9 0.9 %copy-start.3 = (s32[16,16,16]{2,1,0:T(8,128)S(1)}, s32[16,16,16]{2,1,0:T(8,128)}, u32[]{:S(2)}) copy-start(s32[16,16,16]{2,1,0:T(8,128)} %tiles_hbm.1) | copy-start | bytes 49156
  4.8 0.7 copy-start.4
  5.5 0.7 copy-start.5
  6.2 0.7 copy-start.6

commit v4 on v3

--- a/solution.py
+++ b/solution.py
@@ -19,9 +19,12 @@
 SIDE = 4
 QROWS = CAPT // SIDE * HALF
 HROWS = LIVE2 // 2 * HALF
+AHEAD = 4
+RROWS = HROWS // 2
+ROWS = (2, 1, 3, 0)
 ORDER = (
-    (2, 2), (2, 1), (1, 2), (2, 3), (3, 2), (1, 1), (3, 1), (1, 3), (3, 3),
-    (2, 0), (0, 2), (1, 0), (0, 1), (3, 0), (0, 3), (0, 0),
+    (2, 2), (2, 1), (1, 2), (2, 3), (3, 2), (1, 1), (3, 1), (1, 3),
+    (3, 3), (2, 0), (0, 2), (1, 0), (0, 1), (3, 0), (0, 3), (0, 0),
 )
 F32, BF16 = jnp.float32, jnp.bfloat16
 
@@ -122,12 +125,12 @@
 
 
 def kernel(
-    slab, eps_occ, amps_hbm, tiles_hbm, ovov_hbm, ints_hbm, hist_hbm, vir_hbm,
+    slab_hbm, occ_hbm, amps_hbm, tiles_hbm, ovov_hbm, ints_hbm, hist_hbm, vir_hbm,
     new_amps, gram,
-    amps, tiles, vir, codes, jobs, inverse, ints, ovov, hist, stage, a_out, z_land, a_land, a_exp, mask, parts, x_land, y_land, x_sum, y_sum,
+    slab, eps_occ, amps, tiles, vir, codes, jobs, inverse, ints, ovov, hist, stage, a_out, z_land, a_land, a_exp, mask, parts, x_relay, y_relay, x_land, y_land, x_sum, y_sum,
     x_last, y_last, total, cyc, g_one, g_two,
     in_sem, code_sem, zs_send, zs_recv, xy_send, xy_recv, zg_send, zg_recv, fw_send, fw_recv,
-    x_send, x_recv, y_send, y_recv, xl_send, xl_recv, yl_send, yl_recv, g_send, g_recv,
+    xr_send, xr_recv, yr_send, yr_recv, x_send, x_recv, y_send, y_recv, xl_send, xl_recv, yl_send, yl_recv, g_send, g_recv,
 ):
     r = lax.axis_index("reorder")
     p = lax.axis_index("pair")
@@ -147,12 +150,15 @@
     loads = [
         pltpu.make_async_copy(src, dst, in_sem.at[n])
         for n, (src, dst) in enumerate(
-            ((amps_hbm, amps), (tiles_hbm, tiles), (vir_hbm, vir), (ints_hbm, ints), (ovov_hbm, ovov), (hist_hbm, hist))
+            (
+                (amps_hbm, amps), (tiles_hbm, tiles), (vir_hbm, vir), (slab_hbm, slab), (occ_hbm, eps_occ),
+                (ints_hbm, ints), (ovov_hbm, ovov), (hist_hbm, hist),
+            )
         )
     ]
     for load in loads:
         load.start()
-    amps_copy, tiles_copy, vir_copy, w_copy, ovov_copy, hist_copy = loads
+    amps_copy, tiles_copy, vir_copy, slab_copy, occ_copy, w_copy, ovov_copy, hist_copy = loads
 
     def greet(device):
         pl.semaphore_signal(barrier, inc=1, device_id=device, device_id_type=MESH)
@@ -179,38 +185,43 @@
             at = (kk * CAPT + quarter * CAPT // SIDE) * HALF
             a_out[quarter, kk] = stage[at : at + QROWS].astype(BF16)
 
-    pl.semaphore_wait(barrier, NR - 1 + NP - 1)
-
-    def scatter(d):
-        to = (z + d) % SIDE
-        return remote(
-            a_out.at[to], z_land.at[z], zs_send.at[d - 1], zs_recv.at[z], (2 * to + core, p)
-        )
-
-    for d in range(1, SIDE):
-        scatter(d).start()
-    z_land[z] = a_out[z]
-
     tiles_copy.wait()
     vir_copy.wait()
+    slab_copy.wait()
+    occ_copy.wait()
     tables(p, r, tiles, codes)
     code_copy = pltpu.make_async_copy(codes, jobs, code_sem.at[0])
     code_copy.start()
     alive = denominators(p, r, tiles, vir, slab, eps_occ, inverse)
 
-    def turned(d, kk):
-        frm = (z + d) % SIDE
+    pl.semaphore_wait(barrier, NR - 1 + NP - 1)
+
+    def scatter(d):
+        to = (z + d) % SIDE
+        return remote(
+            a_out.at[to], z_land.at[z], zs_send.at[d - 1], zs_recv.at[z], (2 * to + core, p)
+        )
+
+    for d in range(1, SIDE):
+        scatter(d).start()
+    z_land[z] = a_out[z]
+
+    def turned(dy, kk):
+        frm = (y + SIDE - dy) % SIDE
         k = 4 * frm + 2 * core + kk
         return frm, k, remote(
-            z_land.at[frm, kk], a_land.at[p, z], xy_send.at[2 * d + kk], xy_recv.at[p], (r, k)
-        )
-
-    for d in range(SIDE):
-        frm = (z + d) % SIDE
-        if d:
+            z_land.at[frm, kk], a_land.at[p, z], xy_send.at[2 * dy + kk], xy_recv.at[p], (r, k)
+        )
+
+    for dy in ROWS:
+        frm = (y + SIDE - dy) % SIDE
+
+        @pl.when(frm != z)
+        def _():
             arrive(z_land.at[frm], zs_recv.at[frm])
+
         for kk in range(2):
-            frm, k, copy = turned(d, kk)
+            frm, k, copy = turned(dy, kk)
 
             @pl.when(k != p)
             def _():
@@ -232,20 +243,20 @@
             (2 * ((z + e) % SIDE) + core, p),
         )
 
-    @pl.when(main)
-    def _():
-        def step(n, c):
-            i = place_of(n)
-
+    def spread_planes(n):
+        i = place_of(n)
+
+        @pl.when(main)
+        def _():
             @pl.when(i != p)
             def _():
                 arrive(a_land.at[i, z], xy_recv.at[i])
 
-            for e in range(1, SIDE):
+            for e in (2, 1, 3):
                 gather(i, e).start()
-            return c
-
-        lax.fori_loop(0, NP, step, 0)
+
+    for n in range(AHEAD):
+        spread_planes(n)
 
     def forward(i):
         return remote(a_land.at[i], a_land.at[i], fw_send.at[i], fw_recv.at[i], (r + 1 - 2 * core, p))
@@ -331,6 +342,10 @@
         @pl.when(n < NP - 1)
         def _():
             collect(n + 1)
+
+        @pl.when(n < NP - AHEAD)
+        def _():
+            spread_planes(n + AHEAD)
 
         @pl.when(jnp.logical_not(main))
         def _():
@@ -376,11 +391,11 @@
 
         for e in range(1, SIDE):
 
-            @pl.when(n == ORDER.index((e, 0)))
+            @pl.when(n == {1: 11, 2: 9, 3: 13}[e])
             def _(e=e):
                 y_pass(e)
 
-            @pl.when(n == ORDER.index((0, e)))
+            @pl.when(n == {1: 12, 2: 10, 3: 14}[e])
             def _(e=e):
                 x_pass(e)
 
@@ -423,10 +438,11 @@
 
     zero = jnp.zeros((8, 128), F32)
     sums = lax.fori_loop(0, HALF, correlate, (zero,) * (NH + 1), unroll=4)
-    at_row = iota((8, 128), 0)
-    mine = zero
+    at_lane = iota((1, 128), 1)
+    mine = jnp.zeros((1, 128), F32)
     for h, s in enumerate(sums):
-        mine = jnp.where(at_row == h, jnp.sum(s, axis=0, keepdims=True), mine)
+        s = jnp.sum(jnp.sum(s, axis=0, keepdims=True), axis=1, keepdims=True)
+        mine = jnp.where(at_lane == h, s, mine)
 
     def row_copy(d):
         return remote(
@@ -451,6 +467,38 @@
         return c
 
     lax.fori_loop(0, HALF, update, 0, unroll=8)
+
+    for d in range(1, SIDE):
+        scatter(d).wait_send()
+        x_last_copy(d).wait_send()
+        y_last_copy(d).wait_send()
+    for d in range(SIDE):
+        for kk in range(2):
+            frm, k, copy = turned(d, kk)
+
+            @pl.when(k != p)
+            def _():
+                copy.wait_send()
+
+    def sent(i, c):
+        @pl.when(i % SIDE != x)
+        def _():
+            x_copy(i).wait_send()
+
+        @pl.when(i // SIDE != y)
+        def _():
+            y_copy(i).wait_send()
+
+        @pl.when(main)
+        def _():
+            for e in range(1, SIDE):
+                gather(i, e).wait_send()
+            forward(i).wait_send()
+
+        return c
+
+    lax.fori_loop(0, NP, sent, 0)
+
     for d in range(1, NR):
         k = (r + d) % NR
         arrive(g_one.at[k], g_recv.at[k])
@@ -460,44 +508,13 @@
     for d in range(1, NP):
         k = (p + d) % NP
         arrive(g_two.at[k], g_recv.at[NR + k])
-    everyone = jnp.sum(jnp.sum(g_two[...], axis=0), axis=1, keepdims=True)
-    everyone = jnp.broadcast_to(everyone, (8, 128))
-    gram[...] = jnp.where(at_row == NH, jnp.sqrt(everyone), everyone) / (TILE * NP)
+    everyone = jnp.sum(g_two[...], axis=0)
+    gram[...] = jnp.where(at_lane == NH, jnp.sqrt(everyone), everyone) / (TILE * NP)
 
     for d in range(1, NR):
         row_copy(d).wait_send()
     for d in range(1, NP):
         pair_copy(d).wait_send()
-    for d in range(1, SIDE):
-        scatter(d).wait_send()
-        x_last_copy(d).wait_send()
-        y_last_copy(d).wait_send()
-    for d in range(SIDE):
-        for kk in range(2):
-            frm, k, copy = turned(d, kk)
-
-            @pl.when(k != p)
-            def _():
-                copy.wait_send()
-
-    def sent(i, c):
-        @pl.when(i % SIDE != x)
-        def _():
-            x_copy(i).wait_send()
-
-        @pl.when(i // SIDE != y)
-        def _():
-            y_copy(i).wait_send()
-
-        @pl.when(main)
-        def _():
-            for e in range(1, SIDE):
-                gather(i, e).wait_send()
-            forward(i).wait_send()
-
-        return c
-
-    lax.fori_loop(0, NP, sent, 0)
 
 
 def local(amps, tile_index, ovov, cycle_ints, history, slab, eps_occ, eps_vir):
@@ -508,18 +525,19 @@
     ints = ints.transpose(0, 2, 1, 3).reshape(dead, TILE, 128)
 
     vmem = pl.BlockSpec(memory_space=pltpu.VMEM)
-    smem = pl.BlockSpec(memory_space=pltpu.SMEM)
     hbm = pl.BlockSpec(memory_space=pltpu.HBM)
     dma = pltpu.SemaphoreType.DMA
     new_amps, gram = pl.pallas_call(
         kernel,
         out_shape=(
             jax.ShapeDtypeStruct((jdev, capt, area), BF16),
-            jax.ShapeDtypeStruct((8, 128), F32),
+            jax.ShapeDtypeStruct((1, 128), F32),
         ),
-        in_specs=[smem, smem] + [hbm] * 6,
+        in_specs=[hbm] * 8,
         out_specs=(vmem, vmem),
         scratch_shapes=[
+            pltpu.SMEM(slab.shape, jnp.int32),
+            pltpu.SMEM(eps_occ.shape, F32),
             pltpu.VMEM((jdev, capt, area), BF16),
             pltpu.VMEM(tile_index.shape, jnp.int32),
             pltpu.VMEM(eps_vir.shape, F32),
@@ -536,6 +554,8 @@
             pltpu.VMEM((capt, TILE, 128), BF16),
             pltpu.VMEM((3, capt, 128), BF16),
             pltpu.VMEM((NP, LIVE2 * HALF, 128), BF16),
+            pltpu.VMEM((2, SIDE, RROWS, 128), BF16),
+            pltpu.VMEM((2, SIDE, RROWS, 128), BF16),
             pltpu.VMEM((SIDE, SIDE, HROWS, 128), BF16),
             pltpu.VMEM((SIDE, SIDE, HROWS, 128), BF16),
             pltpu.VMEM((SIDE - 1, HROWS, 128), BF16),
@@ -544,9 +564,9 @@
             pltpu.VMEM((SIDE, HROWS, 128), BF16),
             pltpu.VMEM((LIVE2, HALF, 128), F32),
             pltpu.VMEM((2 * capt * HALF, 128), F32),
-            pltpu.VMEM((NR, 8, 128), F32),
-            pltpu.VMEM((NP, 8, 128), F32),
-            dma((6,)),
+            pltpu.VMEM((NR, 1, 128), F32),
+            pltpu.VMEM((NP, 1, 128), F32),
+            dma((8,)),
             dma((1,)),
             dma((SIDE - 1,)),
             dma((SIDE,)),
@@ -556,6 +576,10 @@
             dma((NP, SIDE)),
             dma((NP,)),
             dma((NP,)),
+            dma((2, SIDE)),
+            dma((2, SIDE)),
+            dma((2, SIDE)),
+            dma((2, SIDE)),
             dma((NP,)),
             dma((SIDE, SIDE)),
             dma((NP,)),
@@ -568,10 +592,10 @@
             dma((NR + NP,)),
         ],
         compiler_params=pltpu.CompilerParams(
-            collective_id=0, has_side_effects=True, vmem_limit_bytes=48 << 20
+            collective_id=0, has_side_effects=True, vmem_limit_bytes=60 << 20
         ),
     )(slab, eps_occ, amps[0], tile_index, ovov[0], ints, history[:, 0], eps_vir)
-    return new_amps[None], gram[: NH + 1, 0]
+    return new_amps[None], gram[0, : NH + 1]
 
 
 def solution(mesh):

time: 70.8 us -> 66.3 us (0.936)
  local copies, waits for them, and re-layouts: 7.56 us -> 2.8 us
    unnamed x15 -> x1, local copies, waits for them, and re-layouts: 6.94 us -> 1.67 us
    squeeze x0 -> x1, local copies, waits for them, and re-layouts: none -> 1.13 us  [local(): return (new_amps[None], gram[0, :NH + 1])]
where the time goes in v4:
time: 66.3 us; the launch traced here: 66 us
  Pallas kernels  62.5 us (94%)
  local copies, waits for them, and re-layouts  2.8 us (4%)
    pallas_call x1, Pallas kernels, local(): pl.pallas_call(kernel, out_shape=(jax.ShapeDtypeStruct((jdev, capt, area)...  62.5 us
    unnamed x1, local copies, waits for them, and re-layouts  1.67 us

profile of v4, /device:TPU:1, one launch (start us, length us, event | category | flops | bytes accessed | tf_op | source)
XLA Modules:
  0.0 66.0 jit_solution(15862781149109961786)
XLA Ops:
  0.6 62.5 %shard_map.95 = (bf16[2,16,4096]{2,1,0:T(8,128)(2,1)}, f32[1,128]{1,0:T(1,128)}) custom-call(s32[16]{0:T(128)} %slab_hbm.1, f32[200]{0:T(256)} %occ_hbm.1, bf16[2,16,4096]{2,1,0:T(8,128)(2,1)} %bitcast.17, s32[16,16,16]{2,1,0:T(8,128)} %tiles_hbm.1, bf16[2,16,4096]{2,1,0:T(8,128)(2,1)} %bitcast.18, bf16[625,64,128]{2,1,0:T(8,128)(2,1)} %bitcast.15, ...), custom_call_target="tpu_custom_call" | custom-call | tf_op jit(solution)/shard_map/pallas_call | solution.py:530
  63.2 1.1 %slice_bitcast_fusion = f32[7]{0:T(128)} fusion(f32[1,128]{1,0:T(1,128)} %get-tuple-element.5), kind=kLoop, calls=%fused_computation | loop fusion | bytes 56 | tf_op jit(solution)/shard_map/squeeze | solution.py:598
  64.3 1.7 %copy.12 = bf16[1,2,16,4096]{3,2,1,0:T(8,128)(2,1)} copy(bf16[1,2,16,4096]{3,2,1,0:T(8,128)(2,1)} %bitcast.19) | data formatting | bytes 524288

commit v5 on v4

--- a/solution.py
+++ b/solution.py
@@ -19,13 +19,16 @@
 SIDE = 4
 QROWS = CAPT // SIDE * HALF
 HROWS = LIVE2 // 2 * HALF
-AHEAD = 4
+AHEAD = 6
 RROWS = HROWS // 2
 ROWS = (2, 1, 3, 0)
 ORDER = (
-    (2, 2), (2, 1), (1, 2), (2, 3), (3, 2), (1, 1), (3, 1), (1, 3),
-    (3, 3), (2, 0), (0, 2), (1, 0), (0, 1), (3, 0), (0, 3), (0, 0),
+    (2, 2), (2, 1), (1, 2), (2, 3), (3, 2), (2, 0), (0, 2), (1, 1),
+    (3, 3), (1, 3), (3, 1), (1, 0), (0, 1), (3, 0), (0, 3), (0, 0),
 )
+LAG, FIRST_SHARE = 3, 7
+Y_PASS = {2: 10, 1: 13, 3: 14}
+X_PASS = {2: 11, 1: 14, 3: 15}
 F32, BF16 = jnp.float32, jnp.bfloat16
 
 
@@ -280,38 +283,85 @@
     low_f = (iota((TILE, 128), 1) < TILE).astype(F32)
     keep = (low_f.astype(BF16), (1.0 - low_f).astype(BF16))
     low = iota((HALF, 128), 1) < TILE
+    low_b = iota((TILE, 128), 1) < TILE
+    none = jnp.zeros((TILE, 128), BF16)
 
     w_copy.wait()
     code_copy.wait()
 
-    def x_copy(i):
+    def device(dx, dy):
+        return (r, (y + dy) % SIDE * SIDE + (x + dx) % SIDE)
+
+    def relay(i, side, along_x):
+        first = (0 if along_x else HROWS) + side * RROWS
         xi, yi = i % SIDE, i // SIDE
-        return remote(
-            parts.at[i, pl.ds(0, HROWS)], x_land.at[x, yi], x_send.at[i], x_recv.at[x, yi],
-            (r, y * SIDE + xi),
-        )
-
-    def y_copy(i):
+        line = yi if along_x else xi
+        land, send, recv = (x_relay, xr_send, xr_recv) if along_x else (y_relay, yr_send, yr_recv)
+        step = 1 - 2 * side
+        return remote(
+            parts.at[i, pl.ds(first, RROWS)], land.at[side, line], send.at[side, line], recv.at[side, line],
+            device(step, 0) if along_x else device(0, step),
+        )
+
+    def share(i, side, along_x):
         xi, yi = i % SIDE, i // SIDE
-        return remote(
-            parts.at[i, pl.ds(HROWS, HROWS)], y_land.at[y, xi], y_send.at[i], y_recv.at[y, xi],
-            (r, yi * SIDE + x),
-        )
+        line = yi if along_x else xi
+        land, send, recv = (x_land, x_send, x_recv) if along_x else (y_land, y_send, y_recv)
+        step = 1 - 2 * side
+        return remote(
+            parts.at[i, pl.ds(0 if along_x else HROWS, HROWS)], land.at[side, line], send.at[side, line],
+            recv.at[side, line], device(step, 0) if along_x else device(0, step),
+        )
+
+    def send_relays(i, along_x):
+        away = (i % SIDE - x if along_x else i // SIDE - y) % SIDE
+
+        @pl.when(away == 2)
+        def _():
+            for side in range(2):
+                relay(i, side, along_x).start()
+
+    def send_share(i, along_x):
+        away = (i % SIDE - x if along_x else i // SIDE - y) % SIDE
+        line = i // SIDE if along_x else i % SIDE
+        land, recv = (x_relay, xr_recv) if along_x else (y_relay, yr_recv)
+
+        for side in range(2):
+
+            @pl.when(away == 1 + 2 * side)
+            def _(side=side):
+                arrive(land.at[side, line], recv.at[side, line])
+                first = (0 if along_x else HROWS) + side * RROWS
+                own = parts[i, first : first + RROWS].astype(F32)
+                parts[i, first : first + RROWS] = (own + land[side, line].astype(F32)).astype(BF16)
+                share(i, side, along_x).start()
+
+    def delivered(i, along_x):
+        away = (i % SIDE - x if along_x else i // SIDE - y) % SIDE
+
+        @pl.when(away == 2)
+        def _():
+            for side in range(2):
+                relay(i, side, along_x).wait_send()
+
+        for side in range(2):
+
+            @pl.when(away == 1 + 2 * side)
+            def _(side=side):
+                share(i, side, along_x).wait_send()
 
     def x_total(yi):
         acc = parts[yi * SIDE + x, :HROWS].astype(F32)
-        for e in range(1, SIDE):
-            k = (x + e) % SIDE
-            arrive(x_land.at[k, yi], x_recv.at[k, yi])
-            acc += x_land[k, yi].astype(F32)
+        for side in range(2):
+            arrive(x_land.at[side, yi], x_recv.at[side, yi])
+            acc += x_land[side, yi].astype(F32)
         return acc
 
     def y_total(xi):
         acc = parts[y * SIDE + xi, HROWS:].astype(F32)
-        for e in range(1, SIDE):
-            k = (y + e) % SIDE
-            arrive(y_land.at[k, xi], y_recv.at[k, xi])
-            acc += y_land[k, xi].astype(F32)
+        for side in range(2):
+            arrive(y_land.at[side, xi], y_recv.at[side, xi])
+            acc += y_land[side, xi].astype(F32)
         return acc
 
     def x_last_copy(e):
@@ -335,13 +385,14 @@
         y_last_copy(e).start()
 
     collect(0)
+    collect(1)
 
     def one_first(n, c):
         i = place_of(n)
 
-        @pl.when(n < NP - 1)
-        def _():
-            collect(n + 1)
+        @pl.when(n < NP - 2)
+        def _():
+            collect(n + 2)
 
         @pl.when(n < NP - AHEAD)
         def _():
@@ -366,7 +417,7 @@
                 v = a_exp[tile].reshape(4, CAPT, 128) * mask[sel][None]
                 rows.append(v.reshape(TILE, 128))
                 w = ints[at]
-                cols += [w * keep[0], w * keep[1]]
+                cols += [jnp.where(low_b, w, none), jnp.where(low_b, none, w)]
             out = jnp.dot(
                 jnp.concatenate(rows, axis=1),
                 jnp.concatenate(cols, axis=0),
@@ -381,21 +432,27 @@
 
         lax.fori_loop(0, LIVE2, job, 0, unroll=LIVE2)
 
-        @pl.when(i % SIDE != x)
-        def _():
-            x_copy(i).start()
-
-        @pl.when(i // SIDE != y)
-        def _():
-            y_copy(i).start()
+        send_relays(i, True)
+        send_relays(i, False)
+
+        @pl.when(jnp.logical_and(n >= FIRST_SHARE - LAG, n <= FIRST_SHARE))
+        def _():
+            late = place_of(n - LAG)
+            send_share(late, True)
+            send_share(late, False)
+
+        @pl.when(n >= FIRST_SHARE)
+        def _():
+            send_share(i, True)
+            send_share(i, False)
 
         for e in range(1, SIDE):
 
-            @pl.when(n == {1: 11, 2: 9, 3: 13}[e])
+            @pl.when(n == Y_PASS[e])
             def _(e=e):
                 y_pass(e)
 
-            @pl.when(n == {1: 12, 2: 10, 3: 14}[e])
+            @pl.when(n == X_PASS[e])
             def _(e=e):
                 x_pass(e)
 
@@ -481,13 +538,8 @@
                 copy.wait_send()
 
     def sent(i, c):
-        @pl.when(i % SIDE != x)
-        def _():
-            x_copy(i).wait_send()
-
-        @pl.when(i // SIDE != y)
-        def _():
-            y_copy(i).wait_send()
+        delivered(i, True)
+        delivered(i, False)
 
         @pl.when(main)
         def _():
@@ -556,8 +608,8 @@
             pltpu.VMEM((NP, LIVE2 * HALF, 128), BF16),
             pltpu.VMEM((2, SIDE, RROWS, 128), BF16),
             pltpu.VMEM((2, SIDE, RROWS, 128), BF16),
-            pltpu.VMEM((SIDE, SIDE, HROWS, 128), BF16),
-            pltpu.VMEM((SIDE, SIDE, HROWS, 128), BF16),
+            pltpu.VMEM((2, SIDE, HROWS, 128), BF16),
+            pltpu.VMEM((2, SIDE, HROWS, 128), BF16),
             pltpu.VMEM((SIDE - 1, HROWS, 128), BF16),
             pltpu.VMEM((SIDE - 1, HROWS, 128), BF16),
             pltpu.VMEM((SIDE, HROWS, 128), BF16),
@@ -580,10 +632,10 @@
             dma((2, SIDE)),
             dma((2, SIDE)),
             dma((2, SIDE)),
-            dma((NP,)),
-            dma((SIDE, SIDE)),
-            dma((NP,)),
-            dma((SIDE, SIDE)),
+            dma((2, SIDE)),
+            dma((2, SIDE)),
+            dma((2, SIDE)),
+            dma((2, SIDE)),
             dma((SIDE - 1,)),
             dma((SIDE,)),
             dma((SIDE - 1,)),

time: 66.3 us -> 65.3 us (0.985)
  Pallas kernels: 62.5 us -> 61.6 us
    pallas_call x1, Pallas kernels: 62.5 us -> 61.6 us  [local(): pl.pallas_call(kernel, out_shape=(jax.ShapeDtypeStruct((jdev, capt, area)...]
where the time goes in v5:
time: 65.3 us; the launch traced here: 65.1 us
  Pallas kernels  61.6 us (94%)
  local copies, waits for them, and re-layouts  2.8 us (4%)
    pallas_call x1, Pallas kernels, local(): pl.pallas_call(kernel, out_shape=(jax.ShapeDtypeStruct((jdev, capt, area)...  61.6 us
    unnamed x1, local copies, waits for them, and re-layouts  1.67 us

profile of v5, /device:TPU:1, one launch (start us, length us, event | category | flops | bytes accessed | tf_op | source)
XLA Modules:
  0.0 65.1 jit_solution(6887846817722990471)
XLA Ops:
  0.6 61.6 %shard_map.95 = (bf16[2,16,4096]{2,1,0:T(8,128)(2,1)}, f32[1,128]{1,0:T(1,128)}) custom-call(s32[16]{0:T(128)} %slab_hbm.1, f32[200]{0:T(256)} %occ_hbm.1, bf16[2,16,4096]{2,1,0:T(8,128)(2,1)} %bitcast.17, s32[16,16,16]{2,1,0:T(8,128)} %tiles_hbm.1, bf16[2,16,4096]{2,1,0:T(8,128)(2,1)} %bitcast.18, bf16[625,64,128]{2,1,0:T(8,128)(2,1)} %bitcast.15, ...), custom_call_target="tpu_custom_call" | custom-call | tf_op jit(solution)/shard_map/pallas_call | solution.py:582
  62.3 1.1 %slice_bitcast_fusion = f32[7]{0:T(128)} fusion(f32[1,128]{1,0:T(1,128)} %get-tuple-element.5), kind=kLoop, calls=%fused_computation | loop fusion | bytes 56 | tf_op jit(solution)/shard_map/squeeze | solution.py:650
  63.4 1.7 %copy.12 = bf16[1,2,16,4096]{3,2,1,0:T(8,128)(2,1)} copy(bf16[1,2,16,4096]{3,2,1,0:T(8,128)(2,1)} %bitcast.19) | data formatting | bytes 524288
